TPU v7x, 512 devices: a whole 4x4x16 slice. The times are simulated.
512 devices in a mesh: outer: 64 (over z, y_hi, core), inner: 8 (over y_lo, x).
Axes of the slice: x: 4, y: 4 (y_hi: 2, y_lo: 2; y = y_hi * 2 + y_lo), z: 16, core: 2. Of those that a mesh axis runs over, the one named last changes fastest.
Arguments:
- queries: bfloat16 [131072, 1024], P(('outer', 'inner')), may hold values from -6 to 6
- keys: bfloat16 [131072, 1024], P(('outer', 'inner')), may hold values from -6 to 6
- values: bfloat16 [131072, 1024], P(('outer', 'inner')), may hold values from -6 to 6
Outputs:
- attended: bfloat16 [131072, 1024], P(('outer', 'inner'))
All inputs are finite; a program needn't handle non-finite values.
Results may differ from a plain program's by a relative error of at most 0.0029.
Values may be sent and summed in bfloat16 or wider, within the bound.
No kernel may reach another device: no remote copies, remote signals or barrier semaphores. Data moves between devices by JAX's collectives and lax.ppermute only.
A program may use at most 64 MiB of HBM per device.

v0:
```python
import jax
import jax.numpy as jnp
from jax import lax
from jax.sharding import PartitionSpec as P

HEAD_DIM = 128
SECOND_DILATION = 8
THIRD_DILATION = 64
GROUP = 8


def shortened(value):
    return jax.tree.map(lambda a: a.astype(jnp.bfloat16) if a.dtype == jnp.float32 else a, value)


def attend_head(q_head, k_head, v_head):
    scaling = q_head.shape[1] ** (-0.5)
    scores = (
        lax.dot_general(
            q_head, k_head, (((1,), (1,)), ((), ())), preferred_element_type=jnp.float32
        )
        * scaling
    )
    peak_now = jnp.max(scores, axis=1)
    weights = jnp.exp(scores - peak_now[:, None])
    total_list = jnp.sum(weights, axis=1)
    summed_output = jnp.dot(
        weights.astype(jnp.bfloat16), v_head, preferred_element_type=jnp.float32
    )
    return (peak_now, total_list, summed_output)


def level_stats(queries, keys, values, device_heads):
    head_width = queries.shape[1] // device_heads

    def one_head(head_no):
        start = head_no * head_width
        return attend_head(queries, keys, values)

    peak_now, total_list, summed_output = lax.map(
        one_head, jnp.arange(device_heads, dtype=jnp.int32)
    )
    return (peak_now.T, total_list.T, jnp.swapaxes(summed_output, 0, 1))


def blocked_stats(queries, keys, values, device_heads):
    row_count = queries.shape[0]
    block_rows = min(512, row_count)

    def one_block(block_no):
        piece_q = lax.dynamic_slice_in_dim(queries, block_no * block_rows, block_rows, 0)
        return level_stats(piece_q, keys, values, device_heads)

    current_maximum, total_list, summed_output = lax.map(
        one_block, jnp.arange(row_count // block_rows, dtype=jnp.int32)
    )
    return (
        current_maximum.reshape(row_count, device_heads),
        total_list.reshape(row_count, device_heads),
        summed_output.reshape(row_count, device_heads, -1),
    )


def select_rows(rows, rate, leading_head, device_heads):
    head_width = rows.shape[1] // device_heads
    blocks = rows.shape[0] // rate
    layout = rows.reshape(blocks, rate, device_heads, head_width)
    window = lax.dynamic_slice_in_dim(layout, leading_head, device_heads, 1)
    picked = jnp.diagonal(window, axis1=1, axis2=2)
    return jnp.swapaxes(picked, 1, 2).reshape(blocks, device_heads * head_width)


def merge_level(
    current_maximum, total_list, summed_output, top_add, total_add, sum_add, rate, leading_head
):
    device_heads = current_maximum.shape[1]
    blocks = current_maximum.shape[0] // rate
    head_width = summed_output.shape[2]
    chosen = (
        jnp.arange(rate, dtype=jnp.int32)[:, None]
        == (leading_head + jnp.arange(device_heads, dtype=jnp.int32))[None, :]
    )
    base_top = current_maximum.reshape(blocks, rate, device_heads)
    extra_top = top_add[:, None, :]
    peak_now = jnp.where(chosen, jnp.maximum(base_top, extra_top), base_top)
    near_w = jnp.exp(base_top - peak_now)
    far_w = jnp.where(chosen, jnp.exp(extra_top - peak_now), 0.0)
    new_total = (
        near_w * total_list.reshape(blocks, rate, device_heads) + far_w * total_add[:, None, :]
    )
    new_sum = (
        near_w[..., None] * summed_output.reshape(blocks, rate, device_heads, head_width)
        + far_w[..., None] * sum_add[:, None, :, :]
    )
    return (
        peak_now.reshape(-1, device_heads),
        new_total.reshape(-1, device_heads),
        new_sum.reshape(-1, device_heads, head_width),
    )


def finish_rows(total_list, summed_output):
    return (
        (summed_output / total_list[..., None])
        .reshape(summed_output.shape[0], -1)
        .astype(jnp.bfloat16)
    )


def body(queries, keys, values):
    device_heads = queries.shape[1] // HEAD_DIM // lax.axis_size("inner")
    leading_head = lax.axis_index("inner") * device_heads
    segment_query, segment_key, segment_value = (
        lax.all_to_all(queries, "inner", split_axis=1, concat_axis=0, tiled=True),
        lax.all_to_all(keys, "inner", split_axis=1, concat_axis=0, tiled=True),
        lax.all_to_all(values, "inner", split_axis=1, concat_axis=0, tiled=True),
    )
    current_maximum, total_list, summed_output = blocked_stats(
        segment_query, segment_key, segment_value, device_heads
    )
    middle_query = select_rows(segment_query, SECOND_DILATION, leading_head, device_heads)
    middle_key = select_rows(segment_key, SECOND_DILATION, leading_head, device_heads)
    middle_value = select_rows(segment_value, SECOND_DILATION, leading_head, device_heads)
    distant_query = select_rows(segment_query, THIRD_DILATION, leading_head, device_heads)
    gathered_k, gathered_v = (
        lax.all_gather(shortened(middle_key), "outer", axis=0, tiled=True).astype(middle_key.dtype),
        lax.all_gather(shortened(middle_value), "outer", axis=0, tiled=True).astype(
            middle_value.dtype
        ),
    )
    span_rows = GROUP * middle_key.shape[0]
    own_group = lax.axis_index("outer") // GROUP
    group_k = lax.dynamic_slice_in_dim(gathered_k, own_group * span_rows, span_rows, 0)
    group_v = lax.dynamic_slice_in_dim(gathered_v, own_group * span_rows, span_rows, 0)
    stride = THIRD_DILATION // SECOND_DILATION
    far_k = gathered_k.reshape(-1, stride, gathered_k.shape[1])[:, 0]
    far_v = gathered_v.reshape(-1, stride, gathered_v.shape[1])[:, 0]
    middle_maximum, middle_total, middle_sum = blocked_stats(
        middle_query, group_k, group_v, device_heads
    )
    distant_maximum, distant_total, distant_sum = blocked_stats(
        distant_query, far_k, far_v, device_heads
    )
    current_maximum, total_list, summed_output = merge_level(
        current_maximum,
        total_list,
        summed_output,
        middle_maximum,
        middle_total,
        middle_sum,
        SECOND_DILATION,
        leading_head,
    )
    current_maximum, total_list, summed_output = merge_level(
        current_maximum,
        total_list,
        summed_output,
        distant_maximum,
        distant_total,
        distant_sum,
        THIRD_DILATION,
        leading_head,
    )
    result = finish_rows(total_list, summed_output)
    return lax.all_to_all(result, "inner", split_axis=0, concat_axis=1, tiled=True)


def solution(mesh):
    placed = (P(("outer", "inner"), None), P(("outer", "inner"), None), P(("outer", "inner"), None))
    return jax.shard_map(
        body, mesh=mesh, in_specs=placed, out_specs=P(("outer", "inner"), None), check_vma=False
    )
```

profile of v0, /device:TPU:1, one launch (start us, length us, event | category | flops | bytes accessed | tf_op | source)
XLA Modules:
  0.0 358.3 jit_solution(3632596990225039560)
XLA Ops:
  6.5 2.1 copy.41
  8.6 5.9 %all-to-all-start.1 = ((bf16[256,8,128]{0,2,1:T(8,128)(2,1)}), bf16[256,8,128]{0,2,1:T(8,128)(2,1)S(1)}, u32[]{:S(2)}, u32[]{:S(2)}) async-start(bf16[256,8,128]{0,2,1:T(8,128)(2,1)} %bitcast.7), calls=%async_computation.1 | async-start | bytes 1048576 | tf_op jit(solution)/shard_map/all_to_all | solution.py:115
  14.5 7.5 %all-to-all-done.1 = bf16[256,8,128]{0,2,1:T(8,128)(2,1)S(1)} async-done(((bf16[256,8,128]{0,2,1:T(8,128)(2,1)}), bf16[256,8,128]{0,2,1:T(8,128)(2,1)S(1)}, u32[]{:S(2)}, u32[]{:S(2)}) %all-to-all-start.1) | async-done | bytes 524320 | tf_op jit(solution)/shard_map/all_to_all | solution.py:115
  22.0 0.3 copy.42
  22.3 0.1 constant_dynamic-slice_fusion.2
  22.5 0.6 copy.47
  23.2 1.2 copy.43
  24.4 10.0 %all_to_all.73 = bf16[256,8,128]{0,2,1:T(8,128)(2,1)S(1)} all-to-all(bf16[256,8,128]{0,2,1:T(8,128)(2,1)S(1)} %bitcast.101), channel_id=1, replica_groups=mesh['outer'=64,'inner'=8] {'inner'}, dimensions={1} | all-to-all | bytes 1048576 | tf_op jit(solution)/shard_map/all_to_all | solution.py:116
  34.4 0.3 copy.44
  34.6 0.1 constant_dynamic-slice_fusion
  34.8 0.6 copy.50
  35.5 1.0 copy.39
  36.5 3.5 all-to-all-start
  40.0 0.7 broadcast_in_dim.102
  40.7 0.7 broadcast_in_dim.99
  41.5 6.0 %all-to-all-done = bf16[256,8,128]{0,2,1:T(8,128)(2,1)S(1)} async-done(((bf16[256,8,128]{0,2,1:T(8,128)(2,1)}), bf16[256,8,128]{0,2,1:T(8,128)(2,1)S(1)}, u32[]{:S(2)}, u32[]{:S(2)}) %all-to-all-start) | async-done | bytes 524320 | tf_op jit(solution)/shard_map/all_to_all | solution.py:114
  47.5 0.3 copy.40
  47.8 15.0 %while.22 = (s32[]{:T(128)}, f32[4,512,1]{1,2,0:T(1,128)S(1)}, f32[4,512,1]{1,2,0:T(1,128)S(1)}, f32[4,512,1,128]{3,1,2,0:T(8,128)S(1)}, s32[4]{0:T(128)S(1)}, /...) while((s32[]{:T(128)}, f32[4,512,1]{1,2,0:T(1,128)S(1)}, ...), condition=%wide.region_3.4_spmd, body=%wide.region_0.3_spmd.sunk | while | flops 545258496 | bytes 14041283 | solution.py:54
  47.8 0.6 dynamic_slice.51
  49.1 0.8 multiply_reduce_fusion.2
  49.9 0.8 fusion.70
  50.7 0.8 fusion.71
  51.6 0.6 dynamic_slice.51
  52.8 0.8 multiply_reduce_fusion.2
  53.6 0.8 fusion.70
  54.4 0.8 fusion.71
  55.3 0.6 dynamic_slice.51
  56.5 0.8 multiply_reduce_fusion.2
  57.3 0.8 fusion.70
  58.2 0.9 fusion.71
  59.0 0.6 dynamic_slice.51
  60.3 0.8 multiply_reduce_fusion.2
  61.1 0.8 fusion.70
  61.9 0.8 fusion.71
  62.8 0.6 reshape_reshape.12
  63.4 0.6 reshape_reshape.14
  64.1 0.1 constant_dynamic-slice_fusion.3
  64.2 115.4 %all-gather.5.cloned.1.call-done = bf16[16384,1,1,128]{3,0,2,1:T(8,128)(2,1)} async-done(((bf16[256,1,1,128]{3,0,2,1:T(8,128)(2,1)}), bf16[16384,1,1,128]{3,0,2,1:T(8,128)(2,1)}) %all-gather.5.cloned.1.call-update) | async-done | bytes 4194320 | tf_op jit(solution)/shard_map/all_gather | solution.py:126
  179.7 1.6 fusion.59
  181.3 0.7 max.99
  182.0 2.5 slice.8
  184.5 0.4 fusion.58
  185.1 0.4 copy-done.3
  185.4 0.7 max.97
  186.1 0.1 max.92
  186.2 0.1 max.93
  186.3 0.8 fusion.35
  187.2 0.1 mul.181
  187.3 0.7 mul.183
  188.0 1.1 fusion.16
  189.1 0.7 mul.176
  189.7 0.8 mul.177
  190.5 0.7 mul.178
  191.2 0.8 max.100
  192.0 0.7 max.101
  192.7 135.8 %all-gather.7.cloned.1.call-done = bf16[16384,1,1,128]{3,0,2,1:T(8,128)(2,1)} async-done(((bf16[256,1,1,128]{3,0,2,1:T(8,128)(2,1)}), bf16[16384,1,1,128]{3,0,2,1:T(8,128)(2,1)}) %all-gather.7.cloned.1.call-update) | async-done | bytes 4194320 | tf_op jit(solution)/shard_map/all_gather | solution.py:127
  328.5 2.5 slice.9
  331.0 0.9 fusion.26
  331.9 0.8 fusion.51
  332.7 1.5 fusion.18
  334.4 1.7 fusion.22
  336.2 14.0 %all_to_all.74 = bf16[8,256,128]{2,1,0:T(8,128)(2,1)S(1)} all-to-all(bf16[8,256,128]{2,1,0:T(8,128)(2,1)S(1)} %fusion.22), channel_id=1, replica_groups=mesh['outer'=64,'inner'=8] {'inner'}, dimensions={0} | all-to-all | bytes 1048576 | tf_op jit(solution)/shard_map/all_to_all | solution.py:165
  350.2 0.2 copy.51
  350.4 1.0 copy.52
  (32 shorter events, 0.7 us)
Async XLA Ops:
  6.5 28.9 %copy-start = (bf16[256,1024]{1,0:T(8,128)(2,1)S(1)}, bf16[256,1024]{1,0:T(8,128)(2,1)}, u32[]{:S(2)}) copy-start(bf16[256,1024]{1,0:T(8,128)(2,1)} %param.5) | copy-start | bytes 1572868
  8.6 13.4 %all-to-all-start.1 = ((bf16[256,8,128]{0,2,1:T(8,128)(2,1)}), bf16[256,8,128]{0,2,1:T(8,128)(2,1)S(1)}, u32[]{:S(2)}, u32[]{:S(2)}) async-start(bf16[256,8,128]{0,2,1:T(8,128)(2,1)} %bitcast.7), calls=%async_computation.1 | async-start | bytes 1048576 | tf_op jit(solution)/shard_map/all_to_all | solution.py:115
  14.5 165.2 %all-gather.5.cloned.1.call-start = ((), (), s32[]{:S(2)}) async-start(), calls=%async_computation.4 | async-start | bytes 4259840 | tf_op jit(solution)/shard_map/all_gather | solution.py:126
  23.1 305.4 %all-gather.7.cloned.1.call-start = ((), (), s32[]{:S(2)}) async-start(), calls=%async_computation.5 | async-start | bytes 4259840 | tf_op jit(solution)/shard_map/all_gather | solution.py:127
  36.5 11.0 %all-to-all-start = ((bf16[256,8,128]{0,2,1:T(8,128)(2,1)}), bf16[256,8,128]{0,2,1:T(8,128)(2,1)S(1)}, u32[]{:S(2)}, u32[]{:S(2)}) async-start(bf16[256,8,128]{0,2,1:T(8,128)(2,1)} %bitcast.4), calls=%async_computation | async-start | bytes 1048576 | tf_op jit(solution)/shard_map/all_to_all | solution.py:114
  181.2 3.8 %copy-start.2 = (f32[256]{0:T(256)}, f32[256]{0:T(256)S(1)}, u32[]{:S(2)}) copy-start(f32[256]{0:T(256)S(1)} %get-tuple-element.198) | copy-start | bytes 3076
  184.9 0.5 copy-start.3
  186.2 145.7 %copy-start.1 = (f32[8,256]{1,0:T(8,128)S(1)}, f32[8,256]{1,0:T(8,128)}, u32[]{:S(2)}) copy-start(f32[8,256]{1,0:T(8,128)} %max.97) | copy-start | bytes 24580
Sparse Core Ops, SparseCore 0:
  23.2 156.3 all-gather.4
  182.9 145.5 all-gather.6
where the time goes:
time: 359 us; the launch traced here: 358 us
  waiting for transfers between devices  265 us (74%)
  local copies, waits for them, and re-layouts  24.9 us (7%)
  blocking collectives  24 us (7%)
  between operations  13.7 us (4%)
  matrix products  10.9 us (3%)
  starting transfers between devices  9.43 us (3%)
  other arithmetic  7.78 us (2%)
    all_gather x1, waiting for transfers between devices, body(): lax.all_gather(shortened(middle_value), 'outer', axis=0, tiled=True)  136 us
    all_gather x1, waiting for transfers between devices, body(): lax.all_gather(shortened(middle_key), 'outer', axis=0, tiled=True)  115 us
    all_to_all x1, blocking collectives, body(): lax.all_to_all(result, 'inner', split_axis=0, concat_axis=1, tiled=True)  14 us
    all_to_all x1, blocking collectives, body(): lax.all_to_all(values, 'inner', split_axis=1, concat_axis=0, tiled=True)  9.95 us
    all_to_all x1, waiting for transfers between devices, body(): lax.all_to_all(keys, 'inner', split_axis=1, concat_axis=0, tiled=True)  7.49 us
  transfers between devices with their start and end apart: 4, of which 4 were waited for; matrix products, arithmetic and copies ran while one was open for 9% of the time, Pallas kernels for 0%

commit v1 on v0

v1 whole, which is shorter than its diff:
```python
import functools
import math

import jax
import jax.numpy as jnp
from jax import lax
from jax.experimental import pallas as pl
from jax.experimental.pallas import tpu as pltpu
from jax.sharding import PartitionSpec as P

D = 128
HEADS = 8
ROWS = 256
SLOTS = 32
FAR = 4
NEAR = 8
GROUPS = 8
SCALE = D**-0.5 * math.log2(math.e)
LIMIT = 48 << 20

NT = (((1,), (1,)), ((), ()))
F32 = jnp.float32
BF16 = jnp.bfloat16


def place(t, head):
    u = t >> 3
    return (((t - head) & 7) << 5) + ((u & 7) << 2) + (u >> 3)


def to_order(head):
    p = lax.broadcasted_iota(jnp.int32, (ROWS, ROWS), 0)
    t = lax.broadcasted_iota(jnp.int32, (1, ROWS), 1)
    return jnp.where(p == place(t, head), 1.0, 0.0).astype(BF16)


def from_order(head):
    p = lax.broadcasted_iota(jnp.int32, (ROWS, ROWS), 1)
    t = lax.broadcasted_iota(jnp.int32, (ROWS, 1), 0)
    return jnp.where(p == place(t, head), 1.0, 0.0).astype(BF16)


def dot(a, b):
    return jnp.dot(a, b, preferred_element_type=F32)


def split_kv(q_ref, k_ref, v_ref, kv_ref, q3_ref):
    third = jnp.zeros((HEADS * FAR, D), F32)
    r = lax.broadcasted_iota(jnp.int32, (HEADS * FAR, ROWS), 0)
    t = lax.broadcasted_iota(jnp.int32, (HEADS * FAR, ROWS), 1)
    for h in range(HEADS):
        order = to_order(h)
        cols = slice(h * D, (h + 1) * D)
        both = jnp.concatenate([k_ref[:, cols], v_ref[:, cols]], axis=1)
        out = dot(order, both).astype(BF16)
        kv_ref[h, 0] = out[:, :D]
        kv_ref[h, 1] = out[:, D:]
        pick = jnp.where((t == 64 * (r & 3) + h) & ((r >> 2) == h), 1.0, 0.0).astype(BF16)
        third = third + dot(pick, q_ref[:, cols])
    q3_ref[...] = third.astype(BF16)


def split_q(q_ref, q3_ref, out_ref):
    for h in range(HEADS):
        cols = slice(h * D, (h + 1) * D)
        out_ref[h, :ROWS] = dot(to_order(h), q_ref[:, cols]).astype(BF16)
    a = lax.broadcasted_iota(jnp.int32, (ROWS, ROWS), 0)
    b = lax.broadcasted_iota(jnp.int32, (ROWS, ROWS), 1)
    src = (((a >> 2) & 7) << 5) + ((a >> 5) << 2) + (a & 3)
    moved = dot(jnp.where(b == src, 1.0, 0.0).astype(BF16), q3_ref[...]).astype(BF16)
    for h in range(HEADS):
        out_ref[h, ROWS:] = moved[h * 32 : (h + 1) * 32]


def pick_chosen(kv_ref, kv2_ref, far_ref):
    kv2 = kv_ref[...]
    kv2_ref[...] = kv2
    a = lax.broadcasted_iota(jnp.int32, (HEADS * FAR, ROWS), 0)
    b = lax.broadcasted_iota(jnp.int32, (HEADS * FAR, ROWS), 1)
    pick = jnp.where(b == ((a >> 2) << 5) + (a & 3), 1.0, 0.0).astype(BF16)
    k3 = dot(pick, kv2[:, 0].reshape(ROWS, D)).astype(BF16)
    v3 = dot(pick, kv2[:, 1].reshape(ROWS, D)).astype(BF16)
    for g in range(GROUPS):
        far_ref[g, 0] = k3
        far_ref[g, 1] = v3


def two_parts(q):
    scaled = q.astype(F32) * SCALE
    high = scaled.astype(BF16)
    low = (scaled - high.astype(F32)).astype(BF16)
    return jnp.concatenate([high, low], axis=1)


def twice(k):
    return jnp.concatenate([k, k], axis=1)


def with_ones(v):
    return jnp.concatenate([v, jnp.ones_like(v)], axis=1)


def attend(q, keys, values):
    s = lax.dot_general(q, keys, NT, preferred_element_type=F32)
    top = jnp.max(s, axis=1, keepdims=True)
    w = jnp.exp2(s - top).astype(BF16)
    o = dot(w, values)
    return jnp.broadcast_to(top, (q.shape[0], D)), o[:, D:], o[:, :D]


def first_level(q_ref, kv_ref, o_ref, stat_ref, k_scr, v_scr):
    for s in range(HEADS):
        rows = slice(s * ROWS, (s + 1) * ROWS)
        k_scr[rows, :] = twice(kv_ref[s, 0])
        v_scr[rows, :] = with_ones(kv_ref[s, 1])

    def step(s, _):
        top, total, part = attend(two_parts(q_ref[s, :ROWS]), k_scr[...], v_scr[...])
        o_ref[s] = (part / total).astype(BF16)
        stat_ref[0, s] = top[:SLOTS]
        stat_ref[1, s] = total[:SLOTS]
        stat_ref[2, s] = part[:SLOTS]
        return 0

    lax.fori_loop(0, HEADS, step, 0)


def merge(top_a, total_a, part_a, top_b, total_b, part_b):
    peak = jnp.maximum(top_a, top_b)
    a, b = jnp.exp2(top_a - peak), jnp.exp2(top_b - peak)
    return peak, a * total_a + b * total_b, a * part_a + b * part_b


def later_levels(own_ref, q_ref, q3_ref, here_ref, there_ref, far_ref, stat_ref, o_in, o_ref, third_ref, k_scr, v_scr):
    n = NEAR // 2 * ROWS
    for s in range(NEAR // 2):
        for i, ref in enumerate((here_ref, there_ref)):
            at = i * n + s * ROWS
            k_scr[at : at + ROWS, :] = twice(ref[s, :, 0].reshape(ROWS, D))
            v_scr[at : at + ROWS, :] = with_ones(ref[s, :, 1].reshape(ROWS, D))
    q = two_parts(q_ref[...].reshape(ROWS, D))
    level2 = attend(q, k_scr[...], v_scr[...])
    first = [stat_ref[i].reshape(ROWS, D) for i in range(3)]
    top, total, part = merge(*first, *level2)
    o_ref[...] = (part / total).astype(BF16).reshape(HEADS, SLOTS, D)
    a = lax.broadcasted_iota(jnp.int32, (2 * ROWS, ROWS), 0)
    b = lax.broadcasted_iota(jnp.int32, (2 * ROWS, ROWS), 1)
    src = (((a >> 3) & 7) << 5) + ((a >> 6) << 2) + (a & 3)
    q3 = dot(jnp.where(b == src, 1.0, 0.0).astype(BF16), q3_ref[...].reshape(ROWS, D)).astype(BF16)
    k3, v3 = far_ref[:, 0].reshape(ROWS, D), far_ref[:, 1].reshape(ROWS, D)
    top3, total3, part3 = attend(two_parts(q3), twice(k3), with_ones(v3))
    row = lax.broadcasted_iota(jnp.int32, (HEADS * 8, D), 0) & 7

    def both(x):
        x = x.reshape(HEADS, SLOTS, D)[:, :8].reshape(HEADS * 8, D)
        turned = pltpu.roll(x, 4, 0)
        return jnp.where(row < 4, x, turned)

    mine = [both(x) for x in (top, total, part)]
    for j in range(NEAR):
        rows = slice(j * 64, (j + 1) * 64)
        third = [x[rows] for x in (top3, total3, part3)]
        merged = merge(*mine, *third)
        own = own_ref[0] == j
        t, l, o = [jnp.where(own, x, y) for x, y in zip(merged, third)]
        third_ref[j] = jnp.where(row < 4, o / l, t + jnp.log2(l)).reshape(HEADS, 8, D)


def finish(o_ref, third_ref, out_ref):
    parts = third_ref[...].reshape(NEAR, HEADS * 8, D)
    lse = [pltpu.roll(parts[j], HEADS * 8 - 4, 0) for j in range(NEAR)]
    peak = functools.reduce(jnp.maximum, lse)
    weights = [jnp.exp2(x - peak) for x in lse]
    total = sum(weights)
    merged = sum(w * parts[j] for j, w in enumerate(weights)) / total
    merged = merged.reshape(HEADS, 8, D)
    row = lax.broadcasted_iota(jnp.int32, (16, D), 0)
    for h in range(HEADS):
        head = o_ref[h]
        fixed = jnp.concatenate([merged[h], merged[h]], axis=0).astype(BF16)
        start = jnp.where(row < FAR, fixed, head[:16])
        head = jnp.concatenate([start, head[16:]], axis=0)
        out_ref[:, h * D : (h + 1) * D] = dot(from_order(h), head).astype(BF16)


def vmem(n):
    return [pl.BlockSpec(memory_space=pltpu.VMEM)] * n


def call(kernel, outs, ins, scratch=(), in_specs=None, out_specs=None, aliases=None, flops=0, grid=None):
    shapes = [jax.ShapeDtypeStruct(s, d) for s, d in outs]
    extra = {} if grid is None else {"grid": grid}
    got = pl.pallas_call(
        kernel,
        out_shape=shapes,
        in_specs=in_specs or vmem(len(ins)),
        out_specs=out_specs or vmem(len(outs)),
        scratch_shapes=list(scratch),
        input_output_aliases=aliases or {},
        compiler_params=pltpu.CompilerParams(vmem_limit_bytes=LIMIT),
        cost_estimate=pl.CostEstimate(flops=flops, bytes_accessed=1 << 20, transcendentals=0),
        **extra,
    )(*ins)
    return got if len(outs) > 1 else got[0]


def body(queries, keys, values):
    outer = lax.axis_size("outer")
    groups = outer // NEAR
    near = [[g * NEAR + j for j in range(NEAR)] for g in range(groups)]
    far = [[g * NEAR + j for g in range(groups)] for j in range(NEAR)]
    same_core = [[g * NEAR + 2 * m + c for m in range(NEAR // 2)] for g in range(groups) for c in range(2)]
    wide = [[g * NEAR * HEADS + i for i in range(NEAR * HEADS)] for g in range(groups)]
    own = (lax.axis_index("outer") % NEAR).astype(jnp.int32).reshape(1)

    kv, q3 = call(
        split_kv,
        [((HEADS, 2, ROWS, D), BF16), ((HEADS * FAR, D), BF16)],
        (queries, keys, values),
    )
    q3_near = lax.all_gather(q3, "outer", axis=0, tiled=True, axis_index_groups=near)
    kv = lax.all_to_all(kv, "inner", 0, 0, tiled=True)
    q = call(split_q, [((HEADS, ROWS + 32, D), BF16)], (queries, q3_near))
    q = lax.all_to_all(q, "inner", 0, 0, tiled=True)
    chosen, far_kv = call(
        pick_chosen,
        [((HEADS, 2, SLOTS, D), BF16), ((GROUPS, 2, 32, D), BF16)],
        (kv,),
        grid=(1,),
        in_specs=[pl.BlockSpec((HEADS, 2, SLOTS, D), lambda i: (0, 0, 0, 0))],
        out_specs=[
            pl.BlockSpec((HEADS, 2, SLOTS, D), lambda i: (0, 0, 0, 0)),
            pl.BlockSpec((GROUPS, 2, 32, D), lambda i: (0, 0, 0, 0)),
        ],
    )
    here = lax.all_gather(chosen[None], "outer", axis=0, tiled=True, axis_index_groups=same_core)
    there = lax.ppermute(here, "outer", [(i, i ^ 1) for i in range(outer)])
    far_kv = lax.all_to_all(far_kv, "outer", 0, 0, tiled=True, axis_index_groups=far)
    o, stat = call(
        first_level,
        [((HEADS, ROWS, D), BF16), ((3, HEADS, SLOTS, D), F32)],
        (q, kv),
        scratch=[pltpu.VMEM((HEADS * ROWS, 2 * D), BF16), pltpu.VMEM((HEADS * ROWS, 2 * D), BF16)],
        flops=1 << 33,
    )
    whole = lambda *shape: pl.BlockSpec(shape, lambda i: (0,) * len(shape))
    o, third = call(
        later_levels,
        [((HEADS, ROWS, D), BF16), ((NEAR, HEADS, 8, D), F32)],
        (own, q, q, here, there, far_kv, stat, o),
        scratch=[pltpu.VMEM((HEADS * ROWS, 2 * D), BF16), pltpu.VMEM((HEADS * ROWS, 2 * D), BF16)],
        grid=(1,),
        in_specs=[
            pl.BlockSpec(memory_space=pltpu.SMEM),
            whole(HEADS, SLOTS, D),
            pl.BlockSpec((HEADS, 32, D), lambda i: (0, ROWS // 32, 0)),
            whole(NEAR // 2, HEADS, 2, SLOTS, D),
            whole(NEAR // 2, HEADS, 2, SLOTS, D),
            whole(GROUPS, 2, 32, D),
            whole(3, HEADS, SLOTS, D),
            pl.BlockSpec(memory_space=pl.ANY),
        ],
        out_specs=[whole(HEADS, SLOTS, D), whole(NEAR, HEADS, 8, D)],
        aliases={7: 0},
        flops=1 << 30,
    )
    third = third.reshape(NEAR * HEADS, 8, D)
    third = lax.all_to_all(third, ("outer", "inner"), 0, 0, tiled=True, axis_index_groups=wide)
    o = lax.all_to_all(o, "inner", 0, 0, tiled=True)
    return call(finish, [((ROWS, HEADS * D), BF16)], (o, third))


def solution(mesh):
    rows = P(("outer", "inner"), None)
    return jax.shard_map(body, mesh=mesh, in_specs=(rows, rows, rows), out_specs=rows, check_vma=False)
```

time: 359 us -> 128 us (0.36)
  waiting for transfers between devices: 265 us -> 2.26 us
  blocking collectives: 24 us -> 70.9 us
  starting transfers between devices: 9.43 us -> 31.8 us
  local copies, waits for them, and re-layouts: 24.9 us -> 4.86 us
  Pallas kernels: 0 us -> 17.9 us
  between operations: 13.7 us -> 0.05 us
  matrix products: 10.9 us -> 0 us
  other arithmetic: 7.78 us -> 0 us
    all_gather x2 -> x0, waiting for transfers between devices: 251 us -> none  [the longest x1 136 us: body(): lax.all_gather(shortened(middle_value), 'outer', axis=0, tiled=True)]
    all_gather x0 -> x2, blocking collectives: none -> 41.2 us  [the longest x1 21.9 us: body(): lax.all_gather(q3, 'outer', axis=0, tiled=True, axis_index_groups=near)]
    all_to_all x2 -> x3, starting transfers between devices: 9.36 us -> 27.7 us  [the longest x1 14.5 us: body(): lax.all_to_all(far_kv, 'outer', 0, 0, tiled=True, axis_index_groups=far)]
    pallas_call x0 -> x6, Pallas kernels: none -> 17.9 us  [call(): pl.pallas_call(kernel, out_shape=shapes, in_specs=in_specs or vmem(len(in...]
    all_to_all x2 -> x3, waiting for transfers between devices: 13.5 us -> 2.26 us  [the longest x1 2.25 us: body(): lax.all_to_all(far_kv, 'outer', 0, 0, tiled=True, axis_index_groups=far)]
    dot_general x12 -> x0, matrix products: 10.9 us -> none  [the longest x6 5.82 us: attend_head(): jnp.dot(weights.astype(jnp.bfloat16), v_head, preferred_element_type=jnp....]
    all_to_all x2, blocking collectives: 24 us -> 29.6 us  [the longest x1 18.7 us: body(): lax.all_to_all(third, ('outer', 'inner'), 0, 0, tiled=True, axis_index_gr...]
    reduce_sum x6 -> x0, other arithmetic: 5.19 us -> none  [attend_head(): total_list = jnp.sum(weights, axis=1)]
  transfers between devices with their start and end apart: 4 -> 4, of which waited for: 4 -> 1; matrix products, arithmetic and copies ran while one was open for 9% -> 0% of each run, Pallas kernels for 0% -> 11%
where the time goes in v1:
time: 128 us
  blocking collectives  70.9 us (55%)
  starting transfers between devices  31.8 us (25%)
  Pallas kernels  17.9 us (14%)
  local copies, waits for them, and re-layouts  4.86 us (4%)
  waiting for transfers between devices  2.26 us (2%)
    all_gather x1, blocking collectives, body(): lax.all_gather(q3, 'outer', axis=0, tiled=True, axis_index_groups=near)  21.9 us
    all_gather x1, blocking collectives, body(): lax.all_gather(chosen[None], 'outer', axis=0, tiled=True, axis_index_grou...  19.3 us
    all_to_all x1, blocking collectives, body(): lax.all_to_all(third, ('outer', 'inner'), 0, 0, tiled=True, axis_index_gr...  18.7 us
    pallas_call x6, Pallas kernels, call(): pl.pallas_call(kernel, out_shape=shapes, in_specs=in_specs or vmem(len(in...  17.9 us
    all_to_all x1, starting transfers between devices, body(): lax.all_to_all(far_kv, 'outer', 0, 0, tiled=True, axis_index_groups=far)  14.5 us
    all_to_all x1, blocking collectives, body(): o = lax.all_to_all(o, 'inner', 0, 0, tiled=True)  11 us
    all_to_all x1, starting transfers between devices, body(): q = lax.all_to_all(q, 'inner', 0, 0, tiled=True)  7.27 us
    all_to_all x1, starting transfers between devices, body(): kv = lax.all_to_all(kv, 'inner', 0, 0, tiled=True)  5.99 us
  transfers between devices with their start and end apart: 4, of which 1 were waited for; matrix products, arithmetic and copies ran while one was open for 0% of the time, Pallas kernels for 11%

profile of v1, /device:TPU:1, one launch (start us, length us, event | category | flops | bytes accessed | tf_op | source)
XLA Modules:
  0.0 127.7 jit_solution(16237427694656178416)
XLA Ops:
  0.0 0.0 copy-start
  0.0 1.0 copy-done
  1.0 0.0 copy-start.2
  1.0 1.0 copy-done.2
  2.1 0.0 copy-start.3
  2.1 1.0 copy-done.3
  3.1 1.6 %shard_map.37 = (bf16[8,2,256,128]{3,2,1,0:T(8,128)(2,1)}, bf16[32,128]{1,0:T(8,128)(2,1)S(1)}) custom-call(bf16[256,1024]{1,0:T(8,128)(2,1)S(1)} %copy-done, bf16[256,1024]{1,0:T(8,128)(2,1)S(1)} %copy-done.2, bf16[256,1024]{1,0:T(8,128)(2,1)S(1)} %copy-done.3), custom_call_target="tpu_custom_call" | custom-call | bytes 1048576 | tf_op jit(solution)/shard_map/pallas_call | solution.py:193
  4.7 0.0 copy-start.1
  4.7 6.0 %all-to-all-start.1 = ((bf16[8,2,256,128]{3,2,1,0:T(8,128)(2,1)}), bf16[8,2,256,128]{3,2,1,0:T(8,128)(2,1)S(1)}, u32[]{:S(2)}, u32[]{:S(2)}) async-start(bf16[8,2,256,128]{3,2,1,0:T(8,128)(2,1)} %get-tuple-element.14), calls=%async_computation.1 | async-start | bytes 2097152 | tf_op jit(solution)/shard_map/all_to_all | solution.py:222
  10.7 21.9 %all_gather.6.q3_ref = bf16[256,128]{1,0:T(8,128)(2,1)S(1)} all-gather(bf16[32,128]{1,0:T(8,128)(2,1)S(1)} %get-tuple-element.13), channel_id=1, replica_groups={{0,8,16,24,32,40,48,56},{64,72,80,88,96,104,112,120},{128,136,144,152,1..., dimensions={0}, use_global_device_ids=true | all-gather | bytes 73728 | tf_op jit(solution)/shard_map/all_gather | solution.py:221
  32.6 0.0 copy-done.1
  32.6 1.3 %shard_map.38 = bf16[8,288,128]{2,1,0:T(8,128)(2,1)} custom-call(bf16[256,1024]{1,0:T(8,128)(2,1)S(1)} %copy-done.1, bf16[256,128]{1,0:T(8,128)(2,1)S(1)} %all_gather.6.q3_ref), custom_call_target="tpu_custom_call" | custom-call | bytes 1048576 | tf_op jit(solution)/shard_map/pallas_call | solution.py:193
  33.9 0.0 all-to-all-done.1.kv_ref
  33.9 7.3 %all-to-all-start = ((bf16[8,288,128]{2,1,0:T(8,128)(2,1)}), bf16[8,288,128]{2,1,0:T(8,128)(2,1)S(1)}, u32[]{:S(2)}, u32[]{:S(2)}) async-start(bf16[8,288,128]{2,1,0:T(8,128)(2,1)} %shard_map.38), calls=%async_computation | async-start | bytes 1179648 | tf_op jit(solution)/shard_map/all_to_all | solution.py:224
  41.2 0.8 shard_map.39
  42.0 19.3 %all-gather = bf16[32,2,32,128]{3,2,1,0:T(8,128)(2,1)S(1)} all-gather(bf16[8,2,32,128]{3,2,1,0:T(8,128)(2,1)S(1)} %get-tuple-element.15), channel_id=2, replica_groups={{0,16,32,48},{8,24,40,56},{64,80,96,112},{72,88,104,120},{128,144,160,1..., dimensions={0}, use_global_device_ids=true | all-gather | bytes 655360 | tf_op jit(solution)/shard_map/all_gather | solution.py:236
  61.3 4.1 %collective-permute-start = (bf16[4,8,2,32,128]{4,3,2,1,0:T(8,128)(2,1)S(1)}, bf16[4,8,2,32,128]{4,3,2,1,0:T(8,128)(2,1)S(1)}, u32[]{:S(2)}, u32[]{:S(2)}) collective-permute-start(bf16[4,8,2,32,128]{4,3,2,1,0:T(8,128)(2,1)S(1)} %bitcast.3), channel_id=1, source_target_pairs={{0,8},{8,0},{16,24},{24,16},{32,40},{40,32},{48,56},{56,48},{64,72... | collective-permute-start | bytes 1572872 | tf_op jit(solution)/shard_map/ppermute | solution.py:237
  65.4 0.0 all-to-all-done.q_ref.q3_ref
  65.4 14.5 %all-to-all-start.2 = ((bf16[8,2,32,128]{3,2,1,0:T(8,128)(2,1)}), bf16[8,2,32,128]{3,2,1,0:T(8,128)(2,1)S(1)}, u32[]{:S(2)}, u32[]{:S(2)}) async-start(bf16[8,2,32,128]{3,2,1,0:T(8,128)(2,1)} %get-tuple-element.16), calls=%async_computation.2 | async-start | bytes 262144 | tf_op jit(solution)/shard_map/all_to_all | solution.py:238
  79.8 11.5 %shard_map.40 = (bf16[8,256,128]{2,1,0:T(8,128)(2,1)S(1)}, f32[3,8,32,128]{3,2,1,0:T(8,128)S(1)}) custom-call(bf16[8,288,128]{2,1,0:T(8,128)(2,1)S(1)} %all-to-all-done.q_ref.q3_ref, bf16[8,2,256,128]{3,2,1,0:T(8,128)(2,1)S(1)} %all-to-all-done.1.kv_ref), custom_call_target="tpu_custom_call" | custom-call | flops 8589934592 | bytes 1048576 | tf_op jit(solution)/shard_map/pallas_call | solution.py:193
  91.3 0.0 copy-start.4
  91.3 0.7 copy-done.4
  92.1 2.3 %all-to-all-done.2.far_ref = bf16[8,2,32,128]{3,2,1,0:T(8,128)(2,1)S(1)} async-done(((bf16[8,2,32,128]{3,2,1,0:T(8,128)(2,1)}), bf16[8,2,32,128]{3,2,1,0:T(8,128)(2,1)S(1)}, u32[]{:S(2)}, u32[]{:S(2)}) %all-to-all-start.2) | async-done | bytes 131104 | tf_op jit(solution)/shard_map/all_to_all | solution.py:238
  94.3 0.0 collective-permute-done.there_ref
  94.3 0.0 copy-start.5
  94.3 1.0 copy-done.5
  95.3 1.4 %shard_map.41 = (bf16[8,256,128]{2,1,0:T(8,128)(2,1)S(1)}, f32[8,8,8,128]{3,2,1,0:T(8,128)S(1)}) custom-call(s32[1]{0:T(128)} %bitcast.own_ref, bf16[8,288,128]{2,1,0:T(8,128)(2,1)S(1)} %all-to-all-done.q_ref.q3_ref, bf16[8,288,128]{2,1,0:T(8,128)(2,1)S(1)} %all-to-all-done.q_ref.q3_ref, ...), custom_call_target="tpu_custom_call", output_to_operand_aliasing={{0}: (7, {})} | custom-call | flops 1073741824 | bytes 1048576 | tf_op jit(solution)/shard_map/pallas_call | solution.py:193
  96.7 11.0 %all_to_all.25.o_ref = bf16[8,256,128]{2,1,0:T(8,128)(2,1)S(1)} all-to-all(bf16[8,256,128]{2,1,0:T(8,128)(2,1)S(1)} %get-tuple-element.19), channel_id=1, replica_groups=mesh['outer'=64,'inner'=8] {'inner'}, dimensions={0} | all-to-all | bytes 1048576 | tf_op jit(solution)/shard_map/all_to_all | solution.py:269
  107.7 18.7 %all_to_all.26.third_ref = f32[64,8,128]{2,1,0:T(8,128)S(1)} all-to-all(f32[64,8,128]{2,1,0:T(8,128)S(1)} %bitcast.5), channel_id=1, replica_groups={{0,1,2,3,4,5,6,7,8,9,10,11,12,13,14,15,16,17,18,19,20,21,22,23,24,25,26..., dimensions={0} | all-to-all | bytes 524288 | tf_op jit(solution)/shard_map/all_to_all | solution.py:268
  126.3 1.4 %shard_map.42 = bf16[256,1024]{1,0:T(8,128)(2,1)} custom-call(bf16[8,256,128]{2,1,0:T(8,128)(2,1)S(1)} %all_to_all.25.o_ref, f32[64,8,128]{2,1,0:T(8,128)S(1)} %all_to_all.26.third_ref), custom_call_target="tpu_custom_call" | custom-call | bytes 1048576 | tf_op jit(solution)/shard_map/pallas_call | solution.py:193
Async XLA Ops:
  0.0 1.0 copy-start
  1.0 1.0 copy-start.2
  2.1 1.0 copy-start.3
  4.7 27.9 %copy-start.1 = (bf16[256,1024]{1,0:T(8,128)(2,1)S(1)}, bf16[256,1024]{1,0:T(8,128)(2,1)}, u32[]{:S(2)}) copy-start(bf16[256,1024]{1,0:T(8,128)(2,1)} %q_ref.3) | copy-start | bytes 1572868
  4.7 29.2 %all-to-all-start.1 = ((bf16[8,2,256,128]{3,2,1,0:T(8,128)(2,1)}), bf16[8,2,256,128]{3,2,1,0:T(8,128)(2,1)S(1)}, u32[]{:S(2)}, u32[]{:S(2)}) async-start(bf16[8,2,256,128]{3,2,1,0:T(8,128)(2,1)} %get-tuple-element.14), calls=%async_computation.1 | async-start | bytes 2097152 | tf_op jit(solution)/shard_map/all_to_all | solution.py:222
  33.9 31.5 %all-to-all-start = ((bf16[8,288,128]{2,1,0:T(8,128)(2,1)}), bf16[8,288,128]{2,1,0:T(8,128)(2,1)S(1)}, u32[]{:S(2)}, u32[]{:S(2)}) async-start(bf16[8,288,128]{2,1,0:T(8,128)(2,1)} %shard_map.38), calls=%async_computation | async-start | bytes 1179648 | tf_op jit(solution)/shard_map/all_to_all | solution.py:224
  61.3 33.0 %collective-permute-start = (bf16[4,8,2,32,128]{4,3,2,1,0:T(8,128)(2,1)S(1)}, bf16[4,8,2,32,128]{4,3,2,1,0:T(8,128)(2,1)S(1)}, u32[]{:S(2)}, u32[]{:S(2)}) collective-permute-start(bf16[4,8,2,32,128]{4,3,2,1,0:T(8,128)(2,1)S(1)} %bitcast.3), channel_id=1, source_target_pairs={{0,8},{8,0},{16,24},{24,16},{32,40},{40,32},{48,56},{56,48},{64,72... | collective-permute-start | bytes 1572872 | tf_op jit(solution)/shard_map/ppermute | solution.py:237
  65.4 28.9 %all-to-all-start.2 = ((bf16[8,2,32,128]{3,2,1,0:T(8,128)(2,1)}), bf16[8,2,32,128]{3,2,1,0:T(8,128)(2,1)S(1)}, u32[]{:S(2)}, u32[]{:S(2)}) async-start(bf16[8,2,32,128]{3,2,1,0:T(8,128)(2,1)} %get-tuple-element.16), calls=%async_computation.2 | async-start | bytes 262144 | tf_op jit(solution)/shard_map/all_to_all | solution.py:238
  91.3 0.7 copy-start.4
  94.3 1.0 copy-start.5

commit v2 on v1

v2 whole, which is shorter than its diff:
```python
import functools
import math

import jax
import jax.numpy as jnp
from jax import lax
from jax.experimental import pallas as pl
from jax.experimental.pallas import tpu as pltpu
from jax.sharding import PartitionSpec as P

D = 128
HEADS = 8
ROWS = 256
SLOTS = 32
FAR = 4
NEAR = 8
GROUPS = 8
SCALE = D**-0.5 * math.log2(math.e)
LIMIT = 48 << 20

NT = (((1,), (1,)), ((), ()))
F32 = jnp.float32
BF16 = jnp.bfloat16


def place(t, head):
    u = t >> 3
    return (((t - head) & 7) << 5) + ((u & 7) << 2) + (u >> 3)


def to_order(head):
    p = lax.broadcasted_iota(jnp.int32, (ROWS, ROWS), 0)
    t = lax.broadcasted_iota(jnp.int32, (1, ROWS), 1)
    return jnp.where(p == place(t, head), 1.0, 0.0).astype(BF16)


def from_order(head):
    p = lax.broadcasted_iota(jnp.int32, (ROWS, ROWS), 1)
    t = lax.broadcasted_iota(jnp.int32, (ROWS, 1), 0)
    return jnp.where(p == place(t, head), 1.0, 0.0).astype(BF16)


def dot(a, b):
    return jnp.dot(a, b, preferred_element_type=F32)


def split_heads(q_hbm, k_hbm, v_hbm, qkv_ref, near_ref, q_scr, k_scr, v_scr, sems):
    pairs = ((k_hbm, k_scr), (v_hbm, v_scr), (q_hbm, q_scr))
    copies = [pltpu.make_async_copy(src, dst, sems.at[i]) for i, (src, dst) in enumerate(pairs)]
    for c in copies:
        c.start()
    for c in copies:
        c.wait()
    for h in range(HEADS):
        cols = slice(h * D, (h + 1) * D)
        rows = jnp.concatenate([k_scr[:, cols], v_scr[:, cols], q_scr[:, cols]], axis=1)
        out = dot(to_order(h), rows).astype(BF16)
        for i in range(3):
            qkv_ref[h, i] = out[:, i * D : (i + 1) * D]
        for m in range(NEAR // 2):
            near_ref[m, h, :SLOTS] = out[:SLOTS, :D]
            near_ref[m, h, SLOTS : 2 * SLOTS] = out[:SLOTS, D : 2 * D]
            near_ref[m, h, 2 * SLOTS :] = out[:16, 2 * D :]


def pick_far(here_ref, there_ref, far_ref):
    a = lax.broadcasted_iota(jnp.int32, (HEADS * FAR, ROWS), 0)
    b = lax.broadcasted_iota(jnp.int32, (HEADS * FAR, ROWS), 1)
    pick = jnp.where(b == ((a >> 2) << 5) + (a & 3), 1.0, 0.0).astype(BF16)
    for i, ref in enumerate((here_ref, there_ref)):
        for m in range(NEAR // 2):
            k2 = ref[m, :, :SLOTS].reshape(ROWS, D)
            v2 = ref[m, :, SLOTS : 2 * SLOTS].reshape(ROWS, D)
            got = dot(pick, jnp.concatenate([k2, v2], axis=1)).astype(BF16)
            at = (i * (NEAR // 2) + m) * 32
            far_ref[0, at : at + 32] = got[:, :D]
            far_ref[1, at : at + 32] = got[:, D:]


def two_parts(q):
    scaled = q.astype(F32) * SCALE
    high = scaled.astype(BF16)
    low = (scaled - high.astype(F32)).astype(BF16)
    return jnp.concatenate([high, low], axis=1)


def twice(k):
    return jnp.concatenate([k, k], axis=1)


def with_ones(v):
    return jnp.concatenate([v, jnp.ones_like(v)], axis=1)


def attend(q, keys, values):
    s = lax.dot_general(q, keys, NT, preferred_element_type=F32)
    top = jnp.max(s, axis=1, keepdims=True)
    w = jnp.exp2(s - top).astype(BF16)
    o = dot(w, values)
    return jnp.broadcast_to(top, (q.shape[0], D)), o[:, D:], o[:, :D]


def first_level(qkv_ref, o_ref, stat_ref, k_scr, v_scr):
    for s in range(HEADS):
        rows = slice(s * ROWS, (s + 1) * ROWS)
        k_scr[rows, :] = twice(qkv_ref[s, 0])
        v_scr[rows, :] = with_ones(qkv_ref[s, 1])

    def step(s, _):
        top, total, part = attend(two_parts(qkv_ref[s, 2]), k_scr[...], v_scr[...])
        o_ref[s] = (part / total).astype(BF16)
        stat_ref[0, s] = top[:SLOTS]
        stat_ref[1, s] = total[:SLOTS]
        stat_ref[2, s] = part[:SLOTS]
        return 0

    lax.fori_loop(0, HEADS, step, 0)


def merge(top_a, total_a, part_a, top_b, total_b, part_b):
    peak = jnp.maximum(top_a, top_b)
    a, b = jnp.exp2(top_a - peak), jnp.exp2(top_b - peak)
    return peak, a * total_a + b * total_b, a * part_a + b * part_b


def later_levels(own_ref, q_ref, here_ref, there_ref, far_ref, stat_ref, o_in, o_ref, third_ref, k_scr, v_scr):
    half = NEAR // 2
    for i, ref in enumerate((here_ref, there_ref)):
        for m in range(half):
            at = (i * half + m) * ROWS
            k_scr[at : at + ROWS, :] = twice(ref[m, :, :SLOTS].reshape(ROWS, D))
            v_scr[at : at + ROWS, :] = with_ones(ref[m, :, SLOTS : 2 * SLOTS].reshape(ROWS, D))
    q = two_parts(q_ref[...].reshape(ROWS, D))
    level2 = attend(q, k_scr[...], v_scr[...])
    first = [stat_ref[i].reshape(ROWS, D) for i in range(3)]
    top, total, part = merge(*first, *level2)
    o_ref[...] = (part / total).astype(BF16).reshape(HEADS, SLOTS, D)
    n = half * HEADS * 16
    a = lax.broadcasted_iota(jnp.int32, (n // 2, n), 0)
    b = lax.broadcasted_iota(jnp.int32, (n // 2, n), 1)
    pick = jnp.where(b == ((a >> 3) << 4) + (a & 3), 1.0, 0.0).astype(BF16)
    q3 = [dot(pick, ref[:, :, 2 * SLOTS :].reshape(n, D)) for ref in (here_ref, there_ref)]
    q3 = jnp.concatenate(q3, axis=0)
    level3 = attend(two_parts(q3), twice(far_ref[0]), with_ones(far_ref[1]))
    row = lax.broadcasted_iota(jnp.int32, (HEADS * 8, D), 0) & 7

    def both(x):
        x = x.reshape(HEADS, SLOTS, D)[:, :8].reshape(HEADS * 8, D)
        return jnp.where(row < 4, x, pltpu.roll(x, 4, 0))

    mine = [both(x) for x in (top, total, part)]
    core = own_ref[1]
    for j in range(NEAR):
        third = [x[j * 64 : (j + 1) * 64] for x in level3]
        if j < half:
            merged = merge(*mine, *third)
            third = [jnp.where(own_ref[0] == j, x, y) for x, y in zip(merged, third)]
        t, l, o = third
        at = 2 * j + core if j < half else 2 * (j - half) + 1 - core
        third_ref[at] = jnp.where(row < 4, o / l, t + jnp.log2(l)).reshape(HEADS, 8, D)


def finish(o_ref, third_ref, out_ref):
    parts = third_ref[...].reshape(NEAR, HEADS * 8, D)
    lse = [pltpu.roll(parts[j], HEADS * 8 - 4, 0) for j in range(NEAR)]
    peak = functools.reduce(jnp.maximum, lse)
    weights = [jnp.exp2(x - peak) for x in lse]
    total = sum(weights)
    merged = sum(w * parts[j] for j, w in enumerate(weights)) / total
    merged = merged.reshape(HEADS, 8, D)
    row = lax.broadcasted_iota(jnp.int32, (16, D), 0)
    for h in range(HEADS):
        head = o_ref[h]
        fixed = jnp.concatenate([merged[h], merged[h]], axis=0).astype(BF16)
        start = jnp.where(row < FAR, fixed, head[:16])
        head = jnp.concatenate([start, head[16:]], axis=0)
        out_ref[:, h * D : (h + 1) * D] = dot(from_order(h), head).astype(BF16)


def vmem(n):
    return [pl.BlockSpec(memory_space=pltpu.VMEM)] * n


def call(kernel, outs, ins, scratch=(), in_specs=None, out_specs=None, aliases=None, flops=0, grid=None):
    shapes = [jax.ShapeDtypeStruct(s, d) for s, d in outs]
    extra = {} if grid is None else {"grid": grid}
    got = pl.pallas_call(
        kernel,
        out_shape=shapes,
        in_specs=in_specs or vmem(len(ins)),
        out_specs=out_specs or vmem(len(outs)),
        scratch_shapes=list(scratch),
        input_output_aliases=aliases or {},
        compiler_params=pltpu.CompilerParams(vmem_limit_bytes=LIMIT),
        cost_estimate=pl.CostEstimate(flops=flops, bytes_accessed=1 << 20, transcendentals=0),
        **extra,
    )(*ins)
    return got if len(outs) > 1 else got[0]


def whole(*shape):
    return pl.BlockSpec(shape, lambda i: (0,) * len(shape))


def body(queries, keys, values):
    outer = lax.axis_size("outer")
    groups = outer // NEAR
    half = NEAR // 2
    wide = [[g * NEAR * HEADS + i for i in range(NEAR * HEADS)] for g in range(groups)]
    same_core = [
        [(g * NEAR + 2 * m + c) * HEADS + i for m in range(half) for i in range(HEADS)]
        for g in range(groups)
        for c in range(2)
    ]
    place_in_group = lax.axis_index("outer") % NEAR
    own = jnp.stack([place_in_group // 2, place_in_group % 2]).astype(jnp.int32)
    everywhere = ("outer", "inner")

    qkv, near = call(
        split_heads,
        [((HEADS, 3, ROWS, D), BF16), ((half, HEADS, 80, D), BF16)],
        (queries, keys, values),
        in_specs=[pl.BlockSpec(memory_space=pltpu.HBM)] * 3,
        scratch=[pltpu.VMEM((ROWS, HEADS * D), BF16)] * 3 + [pltpu.SemaphoreType.DMA((3,))],
    )
    near = near.reshape(half * HEADS, 80, D)
    here = lax.all_to_all(near, everywhere, 0, 0, tiled=True, axis_index_groups=same_core)
    here = here.reshape(half, HEADS, 80, D)
    there = lax.ppermute(here, "outer", [(i, i ^ 1) for i in range(outer)])
    qkv = lax.all_to_all(qkv, "inner", 0, 0, tiled=True)
    far = call(pick_far, [((2, NEAR * 32, D), BF16)], (here, there))
    moves = [(g * NEAR + j, (g + j) % groups * NEAR + j) for g in range(groups) for j in range(NEAR)]
    far = lax.ppermute(far, "outer", moves)
    o, stat = call(
        first_level,
        [((HEADS, ROWS, D), BF16), ((3, HEADS, SLOTS, D), F32)],
        (qkv,),
        scratch=[pltpu.VMEM((HEADS * ROWS, 2 * D), BF16), pltpu.VMEM((HEADS * ROWS, 2 * D), BF16)],
        flops=1 << 33,
    )
    o, third = call(
        later_levels,
        [((HEADS, ROWS, D), BF16), ((NEAR, HEADS, 8, D), F32)],
        (own, qkv, here, there, far, stat, o),
        scratch=[pltpu.VMEM((HEADS * ROWS, 2 * D), BF16), pltpu.VMEM((HEADS * ROWS, 2 * D), BF16)],
        grid=(1,),
        in_specs=[
            pl.BlockSpec(memory_space=pltpu.SMEM),
            pl.BlockSpec((HEADS, 1, SLOTS, D), lambda i: (0, 2, 0, 0)),
            whole(half, HEADS, 80, D),
            whole(half, HEADS, 80, D),
            whole(2, NEAR * 32, D),
            whole(3, HEADS, SLOTS, D),
            pl.BlockSpec(memory_space=pl.ANY),
        ],
        out_specs=[whole(HEADS, SLOTS, D), whole(NEAR, HEADS, 8, D)],
        aliases={6: 0},
        flops=1 << 30,
    )
    third = third.reshape(NEAR * HEADS, 8, D)
    third = lax.all_to_all(third, everywhere, 0, 0, tiled=True, axis_index_groups=wide)
    o = lax.all_to_all(o, "inner", 0, 0, tiled=True)
    return call(finish, [((ROWS, HEADS * D), BF16)], (o, third))


def solution(mesh):
    rows = P(("outer", "inner"), None)
    return jax.shard_map(body, mesh=mesh, in_specs=(rows, rows, rows), out_specs=rows, check_vma=False)
```

time: 128 us -> 93.6 us (0.73)
  blocking collectives: 70.9 us -> 48.3 us
  starting transfers between devices: 31.8 us -> 13.1 us
  waiting for transfers between devices: 2.26 us -> 11.4 us
  Pallas kernels: 17.9 us -> 15.8 us
    all_gather x2 -> x0, blocking collectives: 41.2 us -> none  [the longest x1 21.9 us: body(): lax.all_gather(q3, 'outer', axis=0, tiled=True, axis_index_groups=near)]
    all_to_all x3 -> x1, starting transfers between devices: 27.7 us -> 3.58 us  [body(): qkv = lax.all_to_all(qkv, 'inner', 0, 0, tiled=True)]
    all_to_all x1 -> x2, blocking collectives: 18.7 us -> 36.7 us  [the longest x1 20.1 us: body(): lax.all_to_all(near, everywhere, 0, 0, tiled=True, axis_index_groups=same...]
    all_to_all x3 -> x1, waiting for transfers between devices: 2.26 us -> 9.84 us  [body(): qkv = lax.all_to_all(qkv, 'inner', 0, 0, tiled=True)]
    ppermute x0 -> x1, starting transfers between devices: none -> 4.9 us  [body(): far = lax.ppermute(far, 'outer', moves)]
    pallas_call x6 -> x5, Pallas kernels: 17.9 us -> 15.8 us  [call(): pl.pallas_call(kernel, out_shape=shapes, in_specs=in_specs or vmem(len(in...]
    ppermute x1, waiting for transfers between devices: 0.01 us -> 1.59 us  [body(): there = lax.ppermute(here, 'outer', [(i, i ^ 1) for i in range(outer)])]
    unnamed x12 -> x8, local copies, waits for them, and re-layouts: 4.86 us -> 4.27 us
  transfers between devices with their start and end apart: 4 -> 3, of which waited for: 1 -> 2; matrix products, arithmetic and copies ran while one was open for 0% -> 0% of each run, Pallas kernels for 11% -> 13%
where the time goes in v2:
time: 93.6 us; the launch traced here: 93.1 us
  blocking collectives  48.3 us (52%)
  Pallas kernels  15.8 us (17%)
  starting transfers between devices  13.1 us (14%)
  waiting for transfers between devices  11.4 us (12%)
  local copies, waits for them, and re-layouts  4.27 us (5%)
    all_to_all x1, blocking collectives, body(): lax.all_to_all(near, everywhere, 0, 0, tiled=True, axis_index_groups=same...  20.1 us
    all_to_all x1, blocking collectives, body(): lax.all_to_all(third, everywhere, 0, 0, tiled=True, axis_index_groups=wide)  16.7 us
    pallas_call x5, Pallas kernels, call(): pl.pallas_call(kernel, out_shape=shapes, in_specs=in_specs or vmem(len(in...  15.8 us
    all_to_all x1, blocking collectives, body(): o = lax.all_to_all(o, 'inner', 0, 0, tiled=True)  11.6 us
    all_to_all x1, waiting for transfers between devices, body(): qkv = lax.all_to_all(qkv, 'inner', 0, 0, tiled=True)  9.84 us
    ppermute x1, starting transfers between devices, body(): far = lax.ppermute(far, 'outer', moves)  4.9 us
    ppermute x1, starting transfers between devices, body(): there = lax.ppermute(here, 'outer', [(i, i ^ 1) for i in range(outer)])  4.62 us
    unnamed x8, local copies, waits for them, and re-layouts  4.27 us
  transfers between devices with their start and end apart: 3, of which 2 were waited for; matrix products, arithmetic and copies ran while one was open for 0% of the time, Pallas kernels for 13%

profile of v2, /device:TPU:1, one launch (start us, length us, event | category | flops | bytes accessed | tf_op | source)
XLA Modules:
  0.0 93.1 jit_solution(8026551068723801427)
XLA Ops:
  0.0 0.0 copy-start.1
  0.0 1.0 %copy-done.1 = bf16[256,1024]{1,0:T(8,128)(2,1)S(1)} copy-done((bf16[256,1024]{1,0:T(8,128)(2,1)S(1)}, bf16[256,1024]{1,0:T(8,128)(2,1)}, u32[]{:S(2)}) %copy-start.1) | copy-done | bytes 524312
  1.0 0.0 copy-start.2
  1.0 1.0 %copy-done.2 = bf16[256,1024]{1,0:T(8,128)(2,1)S(1)} copy-done((bf16[256,1024]{1,0:T(8,128)(2,1)S(1)}, bf16[256,1024]{1,0:T(8,128)(2,1)}, u32[]{:S(2)}) %copy-start.2) | copy-done | bytes 524312
  2.1 0.0 copy-start.3
  2.1 1.0 %copy-done.3 = bf16[256,1024]{1,0:T(8,128)(2,1)S(1)} copy-done((bf16[256,1024]{1,0:T(8,128)(2,1)S(1)}, bf16[256,1024]{1,0:T(8,128)(2,1)}, u32[]{:S(2)}) %copy-start.3) | copy-done | bytes 524312
  3.1 0.9 shard_map.37
  4.0 0.0 copy-start
  4.0 1.1 %copy-done = bf16[8,3,256,128]{3,2,1,0:T(8,128)(2,1)} copy-done((bf16[8,3,256,128]{3,2,1,0:T(8,128)(2,1)}, bf16[8,3,256,128]{3,2,1,0:T(8,128)(2,1)S(1)}, u32[]{:S(2)}) %copy-start) | copy-done | bytes 1572888
  5.2 20.1 %all_to_all.20 = bf16[32,80,128]{2,1,0:T(8,128)(2,1)S(1)} all-to-all(bf16[32,80,128]{2,1,0:T(8,128)(2,1)S(1)} %bitcast.8), channel_id=1, replica_groups={{0,1,2,3,4,5,6,7,16,17,18,19,20,21,22,23,32,33,34,35,36,37,38,39,48,49,..., dimensions={0} | all-to-all | bytes 1310720 | tf_op jit(solution)/shard_map/all_to_all | solution.py:227
  25.3 3.6 %all-to-all-start = ((bf16[8,3,256,128]{3,2,1,0:T(8,128)(2,1)}), bf16[8,3,256,128]{3,2,1,0:T(8,128)(2,1)S(1)}, u32[]{:S(2)}, u32[]{:S(2)}) async-start(bf16[8,3,256,128]{3,2,1,0:T(8,128)(2,1)} %copy-done), calls=%async_computation | async-start | bytes 3145728 | tf_op jit(solution)/shard_map/all_to_all | solution.py:230
  28.8 4.6 %collective-permute-start = (bf16[4,8,80,128]{3,2,1,0:T(8,128)(2,1)S(1)}, bf16[4,8,80,128]{3,2,1,0:T(8,128)(2,1)S(1)}, u32[]{:S(2)}, u32[]{:S(2)}) collective-permute-start(bf16[4,8,80,128]{3,2,1,0:T(8,128)(2,1)S(1)} %bitcast.5), channel_id=1, source_target_pairs={{0,8},{8,0},{16,24},{24,16},{32,40},{40,32},{48,56},{56,48},{64,72... | collective-permute-start | bytes 1966088 | tf_op jit(solution)/shard_map/ppermute | solution.py:229
  33.5 0.1 pad_add_fusion.own_ref
  33.6 1.6 %collective-permute-done.there_ref = bf16[4,8,80,128]{3,2,1,0:T(8,128)(2,1)S(1)} collective-permute-done((bf16[4,8,80,128]{3,2,1,0:T(8,128)(2,1)S(1)}, bf16[4,8,80,128]{3,2,1,0:T(8,128)(2,1)S(1)}, u32[]{:S(2)}, u32[]{:S(2)}) %collective-permute-start) | collective-permute-done | bytes 655392 | tf_op jit(solution)/shard_map/ppermute | solution.py:229
  35.2 0.3 shard_map.38
  35.5 4.9 %collective-permute-start.1 = (bf16[2,256,128]{2,1,0:T(8,128)(2,1)S(1)}, bf16[2,256,128]{2,1,0:T(8,128)(2,1)S(1)}, u32[]{:S(2)}, u32[]{:S(2)}) collective-permute-start(bf16[2,256,128]{2,1,0:T(8,128)(2,1)S(1)} %shard_map.38), channel_id=1, source_target_pairs={{0,0},{8,72},{16,144},{24,216},{32,288},{40,360},{48,432},{56,504}... | collective-permute-start | bytes 393224 | tf_op jit(solution)/shard_map/ppermute | solution.py:233
  40.4 9.8 %all-to-all-done.qkv_ref.q_ref = bf16[8,3,256,128]{3,2,1,0:T(8,128)(2,1)S(1)} async-done(((bf16[8,3,256,128]{3,2,1,0:T(8,128)(2,1)}), bf16[8,3,256,128]{3,2,1,0:T(8,128)(2,1)S(1)}, u32[]{:S(2)}, u32[]{:S(2)}) %all-to-all-start) | async-done | bytes 1572896 | tf_op jit(solution)/shard_map/all_to_all | solution.py:230
  50.2 11.5 %shard_map.39 = (bf16[8,256,128]{2,1,0:T(8,128)(2,1)S(1)}, f32[3,8,32,128]{3,2,1,0:T(8,128)S(1)}) custom-call(bf16[8,3,256,128]{3,2,1,0:T(8,128)(2,1)S(1)} %all-to-all-done.qkv_ref.q_ref), custom_call_target="tpu_custom_call" | custom-call | flops 8589934592 | bytes 1048576 | tf_op jit(solution)/shard_map/pallas_call | solution.py:187
  61.7 0.0 collective-permute-done.1.far_ref
  61.7 1.8 %shard_map.40 = (bf16[8,256,128]{2,1,0:T(8,128)(2,1)S(1)}, f32[8,8,8,128]{3,2,1,0:T(8,128)S(1)}) custom-call(s32[2]{0:T(128)S(1)} %pad_add_fusion.own_ref, bf16[8,3,256,128]{3,2,1,0:T(8,128)(2,1)S(1)} %all-to-all-done.qkv_ref.q_ref, bf16[4,8,80,128]{3,2,1,0:T(8,128)(2,1)S(1)} %bitcast.7, ...), custom_call_target="tpu_custom_call", output_to_operand_aliasing={{0}: (6, {})} | custom-call | flops 1073741824 | bytes 1048576 | tf_op jit(solution)/shard_map/pallas_call | solution.py:187
  63.5 11.6 %all_to_all.21.o_ref = bf16[8,256,128]{2,1,0:T(8,128)(2,1)S(1)} all-to-all(bf16[8,256,128]{2,1,0:T(8,128)(2,1)S(1)} %get-tuple-element.15), channel_id=1, replica_groups=mesh['outer'=64,'inner'=8] {'inner'}, dimensions={0} | all-to-all | bytes 1048576 | tf_op jit(solution)/shard_map/all_to_all | solution.py:262
  75.1 16.7 %all_to_all.22.third_ref = f32[64,8,128]{2,1,0:T(8,128)S(1)} all-to-all(f32[64,8,128]{2,1,0:T(8,128)S(1)} %bitcast.9), channel_id=1, replica_groups={{0,1,2,3,4,5,6,7,8,9,10,11,12,13,14,15,16,17,18,19,20,21,22,23,24,25,26..., dimensions={0} | all-to-all | bytes 524288 | tf_op jit(solution)/shard_map/all_to_all | solution.py:261
  91.7 1.4 %shard_map.41 = bf16[256,1024]{1,0:T(8,128)(2,1)} custom-call(bf16[8,256,128]{2,1,0:T(8,128)(2,1)S(1)} %all_to_all.21.o_ref, f32[64,8,128]{2,1,0:T(8,128)S(1)} %all_to_all.22.third_ref), custom_call_target="tpu_custom_call" | custom-call | bytes 1048576 | tf_op jit(solution)/shard_map/pallas_call | solution.py:187
Async XLA Ops:
  0.0 1.0 %copy-start.1 = (bf16[256,1024]{1,0:T(8,128)(2,1)S(1)}, bf16[256,1024]{1,0:T(8,128)(2,1)}, u32[]{:S(2)}) copy-start(bf16[256,1024]{1,0:T(8,128)(2,1)} %q_hbm.1) | copy-start | bytes 1572868
  1.0 1.0 %copy-start.2 = (bf16[256,1024]{1,0:T(8,128)(2,1)S(1)}, bf16[256,1024]{1,0:T(8,128)(2,1)}, u32[]{:S(2)}) copy-start(bf16[256,1024]{1,0:T(8,128)(2,1)} %k_hbm.1) | copy-start | bytes 1572868
  2.1 1.0 %copy-start.3 = (bf16[256,1024]{1,0:T(8,128)(2,1)S(1)}, bf16[256,1024]{1,0:T(8,128)(2,1)}, u32[]{:S(2)}) copy-start(bf16[256,1024]{1,0:T(8,128)(2,1)} %v_hbm.1) | copy-start | bytes 1572868
  4.0 1.2 %copy-start = (bf16[8,3,256,128]{3,2,1,0:T(8,128)(2,1)}, bf16[8,3,256,128]{3,2,1,0:T(8,128)(2,1)S(1)}, u32[]{:S(2)}) copy-start(bf16[8,3,256,128]{3,2,1,0:T(8,128)(2,1)S(1)} %get-tuple-element.11) | copy-start | bytes 4718596
  25.3 24.9 %all-to-all-start = ((bf16[8,3,256,128]{3,2,1,0:T(8,128)(2,1)}), bf16[8,3,256,128]{3,2,1,0:T(8,128)(2,1)S(1)}, u32[]{:S(2)}, u32[]{:S(2)}) async-start(bf16[8,3,256,128]{3,2,1,0:T(8,128)(2,1)} %copy-done), calls=%async_computation | async-start | bytes 3145728 | tf_op jit(solution)/shard_map/all_to_all | solution.py:230
  28.8 6.3 %collective-permute-start = (bf16[4,8,80,128]{3,2,1,0:T(8,128)(2,1)S(1)}, bf16[4,8,80,128]{3,2,1,0:T(8,128)(2,1)S(1)}, u32[]{:S(2)}, u32[]{:S(2)}) collective-permute-start(bf16[4,8,80,128]{3,2,1,0:T(8,128)(2,1)S(1)} %bitcast.5), channel_id=1, source_target_pairs={{0,8},{8,0},{16,24},{24,16},{32,40},{40,32},{48,56},{56,48},{64,72... | collective-permute-start | bytes 1966088 | tf_op jit(solution)/shard_map/ppermute | solution.py:229
  35.5 26.2 %collective-permute-start.1 = (bf16[2,256,128]{2,1,0:T(8,128)(2,1)S(1)}, bf16[2,256,128]{2,1,0:T(8,128)(2,1)S(1)}, u32[]{:S(2)}, u32[]{:S(2)}) collective-permute-start(bf16[2,256,128]{2,1,0:T(8,128)(2,1)S(1)} %shard_map.38), channel_id=1, source_target_pairs={{0,0},{8,72},{16,144},{24,216},{32,288},{40,360},{48,432},{56,504}... | collective-permute-start | bytes 393224 | tf_op jit(solution)/shard_map/ppermute | solution.py:233

commit v3 on v2

v3 whole, which is shorter than its diff:
```python
import functools
import math

import jax
import jax.numpy as jnp
from jax import lax
from jax.experimental import pallas as pl
from jax.experimental.pallas import tpu as pltpu
from jax.sharding import PartitionSpec as P

D = 128
HEADS = 8
ROWS = 256
SLOTS = 32
FAR = 4
NEAR = 8
GROUPS = 8
SCALE = D**-0.5 * math.log2(math.e)
LIMIT = 48 << 20

NT = (((1,), (1,)), ((), ()))
F32 = jnp.float32
BF16 = jnp.bfloat16


def place(t, head):
    u = t >> 3
    return (((t - head) & 7) << 5) + ((u & 7) << 2) + (u >> 3)


def to_order(head, places=ROWS):
    p = lax.broadcasted_iota(jnp.int32, (places, ROWS), 0)
    t = lax.broadcasted_iota(jnp.int32, (1, ROWS), 1)
    return jnp.where(p == place(t, head), 1.0, 0.0).astype(BF16)


def from_order(head):
    p = lax.broadcasted_iota(jnp.int32, (ROWS, ROWS), 1)
    t = lax.broadcasted_iota(jnp.int32, (ROWS, 1), 0)
    return jnp.where(p == place(t, head), 1.0, 0.0).astype(BF16)


def dot(a, b):
    return jnp.dot(a, b, preferred_element_type=F32)


def chosen_rows(q_hbm, k_hbm, v_hbm, near_ref, q_scr, k_scr, v_scr, sems):
    pairs = ((k_hbm, k_scr), (v_hbm, v_scr), (q_hbm, q_scr))
    copies = [pltpu.make_async_copy(src, dst, sems.at[i]) for i, (src, dst) in enumerate(pairs)]
    for c in copies:
        c.start()
    for c in copies:
        c.wait()
    for h in range(HEADS):
        cols = slice(h * D, (h + 1) * D)
        rows = jnp.concatenate([k_scr[:, cols], v_scr[:, cols], q_scr[:, cols]], axis=1)
        out = dot(to_order(h, SLOTS), rows).astype(BF16)
        for m in range(NEAR // 2):
            near_ref[m, h, :SLOTS] = out[:, :D]
            near_ref[m, h, SLOTS : 2 * SLOTS] = out[:, D : 2 * D]
            near_ref[m, h, 2 * SLOTS :] = out[:16, 2 * D :]


def split_heads(q_hbm, k_hbm, v_hbm, qkv_hbm, q_scr, k_scr, v_scr, out_scr, in_sems, out_sems):
    pairs = ((k_hbm, k_scr), (v_hbm, v_scr), (q_hbm, q_scr))
    copies = [pltpu.make_async_copy(src, dst, in_sems.at[i]) for i, (src, dst) in enumerate(pairs)]
    for c in copies:
        c.start()
    for c in copies:
        c.wait()
    written = []
    for h in range(HEADS):
        cols = slice(h * D, (h + 1) * D)
        rows = jnp.concatenate([k_scr[:, cols], v_scr[:, cols], q_scr[:, cols]], axis=1)
        out = dot(to_order(h), rows).astype(BF16)
        for i in range(3):
            out_scr[h, i] = out[:, i * D : (i + 1) * D]
        c = pltpu.make_async_copy(out_scr.at[h], qkv_hbm.at[h], out_sems.at[h])
        c.start()
        written.append(c)
    for c in written:
        c.wait()


def pick_far(here_ref, far_ref):
    a = lax.broadcasted_iota(jnp.int32, (HEADS * FAR, ROWS), 0)
    b = lax.broadcasted_iota(jnp.int32, (HEADS * FAR, ROWS), 1)
    pick = jnp.where(b == ((a >> 2) << 5) + (a & 3), 1.0, 0.0).astype(BF16)
    for m in range(NEAR // 2):
        k2 = here_ref[m, :, :SLOTS].reshape(ROWS, D)
        v2 = here_ref[m, :, SLOTS : 2 * SLOTS].reshape(ROWS, D)
        got = dot(pick, jnp.concatenate([k2, v2], axis=1)).astype(BF16)
        far_ref[0, m * 32 : (m + 1) * 32] = got[:, :D]
        far_ref[1, m * 32 : (m + 1) * 32] = got[:, D:]


def two_parts(q):
    scaled = q.astype(F32) * SCALE
    high = scaled.astype(BF16)
    low = (scaled - high.astype(F32)).astype(BF16)
    return jnp.concatenate([high, low], axis=1)


def twice(k):
    return jnp.concatenate([k, k], axis=1)


def with_ones(v):
    return jnp.concatenate([v, jnp.ones_like(v)], axis=1)


def attend(q, keys, values):
    s = lax.dot_general(q, keys, NT, preferred_element_type=F32)
    top = jnp.max(s, axis=1, keepdims=True)
    w = jnp.exp2(s - top).astype(BF16)
    o = dot(w, values)
    return jnp.broadcast_to(top, (q.shape[0], D)), o[:, D:], o[:, :D]


def merge(top_a, total_a, part_a, top_b, total_b, part_b):
    peak = jnp.maximum(top_a, top_b)
    a, b = jnp.exp2(top_a - peak), jnp.exp2(top_b - peak)
    return peak, a * total_a + b * total_b, a * part_a + b * part_b


def two_levels(qkv_ref, here_ref, there_ref, o_ref, lse_ref, k1, v1, k2, v2, s_scr, top_scr, first):
    half = NEAR // 2
    for s in range(HEADS):
        rows = slice(s * ROWS, (s + 1) * ROWS)
        k1[rows, :] = twice(qkv_ref[s, 0])
        v1[rows, :] = with_ones(qkv_ref[s, 1])

    def scores(tile):
        if tile < HEADS:
            q, keys = qkv_ref[tile, 2], k1
        else:
            q, keys = qkv_ref[:, 2, :SLOTS].reshape(ROWS, D), k2
        x = lax.dot_general(two_parts(q), keys[...], NT, preferred_element_type=F32)
        s_scr[tile % 2] = x
        top_scr[tile % 2] = jnp.broadcast_to(jnp.max(x, axis=1, keepdims=True), (ROWS, D))

    def weigh(tile):
        top = top_scr[tile % 2]
        w = jnp.exp2(s_scr[tile % 2] - top[:, :1]).astype(BF16)
        o = dot(w, (v1 if tile < HEADS else v2)[...])
        part, total = o[:, :D], o[:, D:]
        if tile < HEADS:
            o_ref[tile, SLOTS:] = (part[SLOTS:] / total[SLOTS:]).astype(BF16)
            rows = slice(tile * SLOTS, (tile + 1) * SLOTS)
            for i, x in enumerate((top, total, part)):
                first[i, rows] = x[:SLOTS]
        else:
            top, total, part = merge(first[0], first[1], first[2], top, total, part)
            o_ref[:, :SLOTS] = (part / total).astype(BF16).reshape(HEADS, SLOTS, D)
            lse_ref[...] = (top + jnp.log2(total)).reshape(HEADS, SLOTS, D)[:, :8]

    scores(0)
    for i, ref in enumerate((here_ref, there_ref)):
        for m in range(half):
            at = (i * half + m) * ROWS
            k2[at : at + ROWS, :] = twice(ref[m, :, :SLOTS].reshape(ROWS, D))
            v2[at : at + ROWS, :] = with_ones(ref[m, :, SLOTS : 2 * SLOTS].reshape(ROWS, D))
    for tile in range(HEADS + 1):
        if tile < HEADS:
            scores(tile + 1)
        weigh(tile)


def merge_third(lse_ref, third_ref, o_in, o_ref):
    o = o_in[...].astype(F32)
    base = o[:, :8].reshape(HEADS * 8, D)
    parts = [third_ref[j].reshape(HEADS * 8, D) for j in range(NEAR)]
    sums = [lse_ref[...].reshape(HEADS * 8, D)] + [pltpu.roll(x, HEADS * 8 - 4, 0) for x in parts]
    peak = functools.reduce(jnp.maximum, sums)
    weights = [jnp.exp2(x - peak) for x in sums]
    last = sum(w * x for w, x in zip(weights, [base] + parts)) / sum(weights)
    row = lax.broadcasted_iota(jnp.int32, (HEADS * 8, D), 0) & 7
    last = jnp.where(row < FAR, last, base).reshape(HEADS, 8, D)
    o_ref[...] = jnp.concatenate([last, o[:, 8:]], axis=1).astype(BF16)


def third_level(core_ref, here_ref, there_ref, far_a, far_b, third_ref):
    half = NEAR // 2
    n = half * HEADS * 16
    a = lax.broadcasted_iota(jnp.int32, (n // 2, n), 0)
    b = lax.broadcasted_iota(jnp.int32, (n // 2, n), 1)
    pick = jnp.where(b == ((a >> 3) << 4) + (a & 3), 1.0, 0.0).astype(BF16)
    q3 = [dot(pick, ref[:, :, 2 * SLOTS :].reshape(n, D)) for ref in (here_ref, there_ref)]
    q3 = jnp.concatenate(q3, axis=0)
    k3 = jnp.concatenate([far_a[0], far_b[0]], axis=0)
    v3 = jnp.concatenate([far_a[1], far_b[1]], axis=0)
    level3 = attend(two_parts(q3), twice(k3), with_ones(v3))
    row = lax.broadcasted_iota(jnp.int32, (HEADS * 8, D), 0) & 7
    core = core_ref[0]
    for j in range(NEAR):
        t, l, o = [x[j * 64 : (j + 1) * 64] for x in level3]
        at = 2 * j + core if j < half else 2 * (j - half) + 1 - core
        third_ref[at] = jnp.where(row < 4, o / l, t + jnp.log2(l)).reshape(HEADS, 8, D)


def finish(o_ref, out_ref):
    for h in range(HEADS):
        out_ref[:, h * D : (h + 1) * D] = dot(from_order(h), o_ref[h]).astype(BF16)


def vmem(n):
    return [pl.BlockSpec(memory_space=pltpu.VMEM)] * n


def call(kernel, outs, ins, scratch=(), in_specs=None, out_specs=None, aliases=None, flops=0, grid=None, limit=LIMIT):
    shapes = [jax.ShapeDtypeStruct(s, d) for s, d in outs]
    extra = {} if grid is None else {"grid": grid}
    got = pl.pallas_call(
        kernel,
        out_shape=shapes,
        in_specs=in_specs or vmem(len(ins)),
        out_specs=out_specs or vmem(len(outs)),
        scratch_shapes=list(scratch),
        input_output_aliases=aliases or {},
        compiler_params=pltpu.CompilerParams(vmem_limit_bytes=limit),
        cost_estimate=pl.CostEstimate(flops=flops, bytes_accessed=1 << 20, transcendentals=0),
        **extra,
    )(*ins)
    return got if len(outs) > 1 else got[0]


def whole(*shape):
    return pl.BlockSpec(shape, lambda i: (0,) * len(shape))


def body(queries, keys, values):
    outer = lax.axis_size("outer")
    groups = outer // NEAR
    half = NEAR // 2
    near_groups = [[g * NEAR + j for j in range(NEAR)] for g in range(groups)]
    same_core = [
        [(g * NEAR + 2 * m + c) * HEADS + i for m in range(half) for i in range(HEADS)]
        for g in range(groups)
        for c in range(2)
    ]
    core = (lax.axis_index("outer") % 2).astype(jnp.int32).reshape(1)
    anywhere = pl.BlockSpec(memory_space=pl.ANY)
    block = pltpu.VMEM((ROWS, HEADS * D), BF16)

    near = call(
        chosen_rows,
        [((half, HEADS, 80, D), BF16)],
        (queries, keys, values),
        in_specs=[anywhere] * 3,
        scratch=[block] * 3 + [pltpu.SemaphoreType.DMA((3,))],
        limit=60 << 20,
    )
    near = near.reshape(half * HEADS, 80, D)
    here = lax.all_to_all(near, ("outer", "inner"), 0, 0, tiled=True, axis_index_groups=same_core)
    here = here.reshape(half, HEADS, 80, D)
    there = lax.ppermute(here, "outer", [(i, i ^ 1) for i in range(outer)])
    qkv = call(
        split_heads,
        [((HEADS, 3, ROWS, D), BF16)],
        (queries, keys, values),
        in_specs=[anywhere] * 3,
        out_specs=[anywhere],
        scratch=[block] * 3
        + [pltpu.VMEM((HEADS, 3, ROWS, D), BF16), pltpu.SemaphoreType.DMA((3,)), pltpu.SemaphoreType.DMA((HEADS,))],
        limit=60 << 20,
    )
    qkv = lax.all_to_all(qkv, "inner", 0, 0, tiled=True)
    far = call(pick_far, [((2, half * 32, D), BF16)], (here,))
    place = [(g, j) for g in range(groups) for j in range(NEAR)]
    far_a, far_b = [
        lax.ppermute(far, "outer", [(g * NEAR + j, (g + j // 2 + by) % groups * NEAR + j) for g, j in place])
        for by in (0, groups // 2)
    ]
    third = call(
        third_level,
        [((NEAR, HEADS, 8, D), F32)],
        (core, here, there, far_a, far_b),
        in_specs=[pl.BlockSpec(memory_space=pltpu.SMEM)] + vmem(4),
        flops=1 << 28,
    )
    third = lax.all_to_all(third, "outer", 0, 0, tiled=True, axis_index_groups=near_groups)
    o, lse = call(
        two_levels,
        [((HEADS, ROWS, D), BF16), ((HEADS, 8, D), F32)],
        (qkv, here, there),
        scratch=[pltpu.VMEM((HEADS * ROWS, 2 * D), BF16)] * 4
        + [pltpu.VMEM((2, ROWS, HEADS * ROWS), F32), pltpu.VMEM((2, ROWS, D), F32), pltpu.VMEM((3, ROWS, D), F32)],
        flops=1 << 33,
    )
    o = call(
        merge_third,
        [((HEADS, ROWS, D), BF16)],
        (lse, third, o),
        grid=(1,),
        in_specs=[whole(HEADS, 8, D), whole(NEAR, HEADS, 8, D), whole(HEADS, 16, D)],
        out_specs=[whole(HEADS, 16, D)],
        aliases={2: 0},
    )
    o = lax.all_to_all(o, "inner", 0, 0, tiled=True)
    return call(finish, [((ROWS, HEADS * D), BF16)], (o,))


def solution(mesh):
    rows = P(("outer", "inner"), None)
    return jax.shard_map(body, mesh=mesh, in_specs=(rows, rows, rows), out_specs=rows, check_vma=False)
```

time: 93.6 us -> 82.9 us (0.89); the launches traced: 93.1 us -> 81.3 us
  blocking collectives: 48.3 us -> 13.7 us
  starting transfers between devices: 13.1 us -> 42.1 us
  local copies, waits for them, and re-layouts: 4.27 us -> 1.09 us
  Pallas kernels: 15.8 us -> 14.1 us
  waiting for transfers between devices: 11.4 us -> 10.2 us
    all_to_all x2 -> x0, blocking collectives: 36.7 us -> none  [the longest x1 20.1 us: body(): lax.all_to_all(near, everywhere, 0, 0, tiled=True, axis_index_groups=same...]
    all_to_all x0 -> x2, starting transfers between devices: none -> 18.3 us  [the longest x1 9.24 us: body(): lax.all_to_all(near, ('outer', 'inner'), 0, 0, tiled=True, axis_index_gro...]
    ppermute x1 -> x2, starting transfers between devices: 4.9 us -> 15.2 us  [body(): lax.ppermute(far, 'outer', [(g * NEAR + j, (g + j // 2 + by) % groups * N...]
    all_to_all x1, waiting for transfers between devices: 9.84 us -> 0.01 us  [body(): qkv = lax.all_to_all(qkv, 'inner', 0, 0, tiled=True)]
    all_to_all x0 -> x2, waiting for transfers between devices: none -> 7.7 us  [the longest x1 7.69 us: body(): lax.all_to_all(near, ('outer', 'inner'), 0, 0, tiled=True, axis_index_gro...]
    unnamed x8 -> x4, local copies, waits for them, and re-layouts: 4.27 us -> 1.09 us
    ppermute x1 -> x2, waiting for transfers between devices: 0.01 us -> 2.53 us  [body(): lax.ppermute(far, 'outer', [(g * NEAR + j, (g + j // 2 + by) % groups * N...]
    all_to_all x1, blocking collectives: 11.6 us -> 13.7 us  [body(): o = lax.all_to_all(o, 'inner', 0, 0, tiled=True)]
  transfers between devices with their start and end apart: 3 -> 6, of which waited for: 2 -> 2; matrix products, arithmetic and copies ran while one was open for 0% -> 0% of each run, Pallas kernels for 13% -> 12%
where the time goes in v3:
time: 82.9 us; the launch traced here: 81.3 us
  starting transfers between devices  42.1 us (51%)
  Pallas kernels  14.1 us (17%)
  blocking collectives  13.7 us (17%)
  waiting for transfers between devices  10.2 us (12%)
  local copies, waits for them, and re-layouts  1.09 us (1%)
    ppermute x2, starting transfers between devices, body(): lax.ppermute(far, 'outer', [(g * NEAR + j, (g + j // 2 + by) % groups * N...  15.2 us
    pallas_call x7, Pallas kernels, call(): pl.pallas_call(kernel, out_shape=shapes, in_specs=in_specs or vmem(len(in...  14.1 us
    all_to_all x1, blocking collectives, body(): o = lax.all_to_all(o, 'inner', 0, 0, tiled=True)  13.7 us
    all_to_all x1, starting transfers between devices, body(): lax.all_to_all(near, ('outer', 'inner'), 0, 0, tiled=True, axis_index_gro...  9.24 us
    all_to_all x1, starting transfers between devices, body(): lax.all_to_all(third, 'outer', 0, 0, tiled=True, axis_index_groups=near_g...  9.04 us
    all_to_all x1, waiting for transfers between devices, body(): lax.all_to_all(near, ('outer', 'inner'), 0, 0, tiled=True, axis_index_gro...  7.69 us
    ppermute x1, starting transfers between devices, body(): there = lax.ppermute(here, 'outer', [(i, i ^ 1) for i in range(outer)])  5.12 us
    all_to_all x1, starting transfers between devices, body(): qkv = lax.all_to_all(qkv, 'inner', 0, 0, tiled=True)  3.58 us
  transfers between devices with their start and end apart: 6, of which 2 were waited for; matrix products, arithmetic and copies ran while one was open for 0% of the time, Pallas kernels for 12%

profile of v3, /device:TPU:1, one launch (start us, length us, event | category | flops | bytes accessed | tf_op | source)
XLA Modules:
  0.0 81.3 jit_solution(6034851625819063628)
XLA Ops:
  0.0 2.6 %shard_map.38 = bf16[4,8,80,128]{3,2,1,0:T(8,128)(2,1)} custom-call(bf16[256,1024]{1,0:T(8,128)(2,1)} %q_hbm.3, bf16[256,1024]{1,0:T(8,128)(2,1)} %k_hbm.3, bf16[256,1024]{1,0:T(8,128)(2,1)} %v_hbm.3), custom_call_target="tpu_custom_call" | custom-call | bytes 1048576 | tf_op jit(solution)/shard_map/pallas_call | solution.py:213
  2.6 9.2 %all-to-all-start.1 = ((bf16[32,80,128]{2,1,0:T(8,128)(2,1)}), bf16[32,80,128]{2,1,0:T(8,128)(2,1)S(1)}, u32[]{:S(2)}, u32[]{:S(2)}) async-start(bf16[32,80,128]{2,1,0:T(8,128)(2,1)} %bitcast.7), calls=%async_computation.1 | async-start | bytes 1310720 | tf_op jit(solution)/shard_map/all_to_all | solution.py:254
  11.9 2.9 %shard_map.37 = bf16[8,3,256,128]{3,2,1,0:T(8,128)(2,1)} custom-call(bf16[256,1024]{1,0:T(8,128)(2,1)} %q_hbm.3, bf16[256,1024]{1,0:T(8,128)(2,1)} %k_hbm.3, bf16[256,1024]{1,0:T(8,128)(2,1)} %v_hbm.3), custom_call_target="tpu_custom_call" | custom-call | bytes 1048576 | tf_op jit(solution)/shard_map/pallas_call | solution.py:213
  14.8 7.7 %all-to-all-done.1 = bf16[32,80,128]{2,1,0:T(8,128)(2,1)S(1)} async-done(((bf16[32,80,128]{2,1,0:T(8,128)(2,1)}), bf16[32,80,128]{2,1,0:T(8,128)(2,1)S(1)}, u32[]{:S(2)}, u32[]{:S(2)}) %all-to-all-start.1) | async-done | bytes 655392 | tf_op jit(solution)/shard_map/all_to_all | solution.py:254
  22.5 3.6 %all-to-all-start = ((bf16[8,3,256,128]{3,2,1,0:T(8,128)(2,1)}), bf16[8,3,256,128]{3,2,1,0:T(8,128)(2,1)S(1)}, u32[]{:S(2)}, u32[]{:S(2)}) async-start(bf16[8,3,256,128]{3,2,1,0:T(8,128)(2,1)} %shard_map.37), calls=%async_computation | async-start | bytes 3145728 | tf_op jit(solution)/shard_map/all_to_all | solution.py:267
  26.1 5.1 %collective-permute-start = (bf16[4,8,80,128]{3,2,1,0:T(8,128)(2,1)S(1)}, bf16[4,8,80,128]{3,2,1,0:T(8,128)(2,1)S(1)}, u32[]{:S(2)}, u32[]{:S(2)}) collective-permute-start(bf16[4,8,80,128]{3,2,1,0:T(8,128)(2,1)S(1)} %bitcast.3), channel_id=1, source_target_pairs={{0,8},{8,0},{16,24},{24,16},{32,40},{40,32},{48,56},{56,48},{64,72... | collective-permute-start | bytes 1966088 | tf_op jit(solution)/shard_map/ppermute | solution.py:256
  31.2 0.2 shard_map.40
  31.4 0.7 collective-permute-start.1
  32.1 14.5 %collective-permute-start.2 = (bf16[2,128,128]{2,1,0:T(8,128)(2,1)S(1)}, bf16[2,128,128]{2,1,0:T(8,128)(2,1)S(1)}, u32[]{:S(2)}, u32[]{:S(2)}) collective-permute-start(bf16[2,128,128]{2,1,0:T(8,128)(2,1)S(1)} %shard_map.40), channel_id=1, source_target_pairs={{0,256},{8,264},{16,336},{24,344},{32,416},{40,424},{48,496},{56,5... | collective-permute-start | bytes 196616 | tf_op jit(solution)/shard_map/ppermute | solution.py:271
  46.6 0.0 collective-permute-done.1.far_a
  46.6 2.5 %collective-permute-done.2.far_b = bf16[2,128,128]{2,1,0:T(8,128)(2,1)S(1)} collective-permute-done((bf16[2,128,128]{2,1,0:T(8,128)(2,1)S(1)}, bf16[2,128,128]{2,1,0:T(8,128)(2,1)S(1)}, u32[]{:S(2)}, u32[]{:S(2)}) %collective-permute-start.2) | collective-permute-done | bytes 65568 | tf_op jit(solution)/shard_map/ppermute | solution.py:271
  49.1 0.0 collective-permute-done.there_ref
  49.1 0.0 copy-start
  49.1 1.3 %shard_map.41 = f32[8,8,8,128]{3,2,1,0:T(8,128)} custom-call(s32[1]{0:T(128)} %bitcast.2.core_ref, bf16[4,8,80,128]{3,2,1,0:T(8,128)(2,1)S(1)} %bitcast.5, bf16[4,8,80,128]{3,2,1,0:T(8,128)(2,1)S(1)} %collective-permute-done.there_ref, bf16[2,128,128]{2,1,0:T(8,128)(2,1)S(1)} %collective-permute-done.1.far_a, ...), custom_call_target="tpu_custom_call" | custom-call | flops 268435456 | bytes 1048576 | tf_op jit(solution)/shard_map/pallas_call | solution.py:213
  50.5 0.0 all-to-all-done.qkv_ref
  50.5 0.0 copy-done
  50.5 9.0 %all-to-all-start.2 = ((f32[8,8,8,128]{3,2,1,0:T(8,128)}), f32[8,8,8,128]{3,2,1,0:T(8,128)S(1)}, u32[]{:S(2)}, u32[]{:S(2)}) async-start(f32[8,8,8,128]{3,2,1,0:T(8,128)} %shard_map.41), calls=%async_computation.2 | async-start | bytes 524288 | tf_op jit(solution)/shard_map/all_to_all | solution.py:281
  59.5 0.0 copy-start.1
  59.5 1.1 %copy-done.1 = bf16[4,8,80,128]{3,2,1,0:T(8,128)(2,1)S(1)} copy-done((bf16[4,8,80,128]{3,2,1,0:T(8,128)(2,1)S(1)}, bf16[4,8,80,128]{3,2,1,0:T(8,128)(2,1)}, u32[]{:S(2)}) %copy-start.1) | copy-done | bytes 655384
  60.6 5.6 %shard_map.39 = (bf16[8,256,128]{2,1,0:T(8,128)(2,1)S(1)}, f32[8,8,128]{2,1,0:T(8,128)S(1)}) custom-call(bf16[8,3,256,128]{3,2,1,0:T(8,128)(2,1)S(1)} %all-to-all-done.qkv_ref, bf16[4,8,80,128]{3,2,1,0:T(8,128)(2,1)S(1)} %bitcast.6, bf16[4,8,80,128]{3,2,1,0:T(8,128)(2,1)S(1)} %copy-done.1), custom_call_target="tpu_custom_call" | custom-call | flops 8589934592 | bytes 1048576 | tf_op jit(solution)/shard_map/pallas_call | solution.py:213
  66.2 0.0 all-to-all-done.2.third_ref
  66.3 0.1 shard_map.42
  66.4 13.7 %all_to_all.20.o_ref = bf16[8,256,128]{2,1,0:T(8,128)(2,1)S(1)} all-to-all(bf16[8,256,128]{2,1,0:T(8,128)(2,1)S(1)} %shard_map.42), channel_id=1, replica_groups=mesh['outer'=64,'inner'=8] {'inner'}, dimensions={0} | all-to-all | bytes 1048576 | tf_op jit(solution)/shard_map/all_to_all | solution.py:299
  80.0 1.3 %shard_map.43 = bf16[256,1024]{1,0:T(8,128)(2,1)} custom-call(bf16[8,256,128]{2,1,0:T(8,128)(2,1)S(1)} %all_to_all.20.o_ref), custom_call_target="tpu_custom_call" | custom-call | bytes 1048576 | tf_op jit(solution)/shard_map/pallas_call | solution.py:213
Async XLA Ops:
  2.6 19.9 %all-to-all-start.1 = ((bf16[32,80,128]{2,1,0:T(8,128)(2,1)}), bf16[32,80,128]{2,1,0:T(8,128)(2,1)S(1)}, u32[]{:S(2)}, u32[]{:S(2)}) async-start(bf16[32,80,128]{2,1,0:T(8,128)(2,1)} %bitcast.7), calls=%async_computation.1 | async-start | bytes 1310720 | tf_op jit(solution)/shard_map/all_to_all | solution.py:254
  22.5 28.0 %all-to-all-start = ((bf16[8,3,256,128]{3,2,1,0:T(8,128)(2,1)}), bf16[8,3,256,128]{3,2,1,0:T(8,128)(2,1)S(1)}, u32[]{:S(2)}, u32[]{:S(2)}) async-start(bf16[8,3,256,128]{3,2,1,0:T(8,128)(2,1)} %shard_map.37), calls=%async_computation | async-start | bytes 3145728 | tf_op jit(solution)/shard_map/all_to_all | solution.py:267
  26.1 23.1 %collective-permute-start = (bf16[4,8,80,128]{3,2,1,0:T(8,128)(2,1)S(1)}, bf16[4,8,80,128]{3,2,1,0:T(8,128)(2,1)S(1)}, u32[]{:S(2)}, u32[]{:S(2)}) collective-permute-start(bf16[4,8,80,128]{3,2,1,0:T(8,128)(2,1)S(1)} %bitcast.3), channel_id=1, source_target_pairs={{0,8},{8,0},{16,24},{24,16},{32,40},{40,32},{48,56},{56,48},{64,72... | collective-permute-start | bytes 1966088 | tf_op jit(solution)/shard_map/ppermute | solution.py:256
  31.4 15.2 %collective-permute-start.1 = (bf16[2,128,128]{2,1,0:T(8,128)(2,1)S(1)}, bf16[2,128,128]{2,1,0:T(8,128)(2,1)S(1)}, u32[]{:S(2)}, u32[]{:S(2)}) collective-permute-start(bf16[2,128,128]{2,1,0:T(8,128)(2,1)S(1)} %shard_map.40), channel_id=1, source_target_pairs={{0,0},{8,8},{16,80},{24,88},{32,160},{40,168},{48,240},{56,248},{6... | collective-permute-start | bytes 196616 | tf_op jit(solution)/shard_map/ppermute | solution.py:271
  32.1 17.1 %collective-permute-start.2 = (bf16[2,128,128]{2,1,0:T(8,128)(2,1)S(1)}, bf16[2,128,128]{2,1,0:T(8,128)(2,1)S(1)}, u32[]{:S(2)}, u32[]{:S(2)}) collective-permute-start(bf16[2,128,128]{2,1,0:T(8,128)(2,1)S(1)} %shard_map.40), channel_id=1, source_target_pairs={{0,256},{8,264},{16,336},{24,344},{32,416},{40,424},{48,496},{56,5... | collective-permute-start | bytes 196616 | tf_op jit(solution)/shard_map/ppermute | solution.py:271
  49.1 1.3 %copy-start = (bf16[4,8,80,128]{3,2,1,0:T(8,128)(2,1)}, bf16[4,8,80,128]{3,2,1,0:T(8,128)(2,1)S(1)}, u32[]{:S(2)}) copy-start(bf16[4,8,80,128]{3,2,1,0:T(8,128)(2,1)S(1)} %collective-permute-done.there_ref) | copy-start | bytes 1966084
  50.5 15.8 %all-to-all-start.2 = ((f32[8,8,8,128]{3,2,1,0:T(8,128)}), f32[8,8,8,128]{3,2,1,0:T(8,128)S(1)}, u32[]{:S(2)}, u32[]{:S(2)}) async-start(f32[8,8,8,128]{3,2,1,0:T(8,128)} %shard_map.41), calls=%async_computation.2 | async-start | bytes 524288 | tf_op jit(solution)/shard_map/all_to_all | solution.py:281
  59.5 1.1 %copy-start.1 = (bf16[4,8,80,128]{3,2,1,0:T(8,128)(2,1)S(1)}, bf16[4,8,80,128]{3,2,1,0:T(8,128)(2,1)}, u32[]{:S(2)}) copy-start(bf16[4,8,80,128]{3,2,1,0:T(8,128)(2,1)} %copy-done) | copy-start | bytes 1966084

commit v4 on v3

--- a/solution.py
+++ b/solution.py
@@ -82,16 +82,21 @@
         c.wait()
 
 
-def pick_far(here_ref, far_ref):
+def pick_chosen(near_ref, far_ref, q3_ref, kv_ref):
+    kv_ref[...] = near_ref[:, :, : 2 * SLOTS]
     a = lax.broadcasted_iota(jnp.int32, (HEADS * FAR, ROWS), 0)
     b = lax.broadcasted_iota(jnp.int32, (HEADS * FAR, ROWS), 1)
     pick = jnp.where(b == ((a >> 2) << 5) + (a & 3), 1.0, 0.0).astype(BF16)
+    pick16 = jnp.where(b[:, : ROWS // 2] == ((a[:, : ROWS // 2] >> 2) << 4) + (a[:, : ROWS // 2] & 3), 1.0, 0.0)
+    pick16 = pick16.astype(BF16)
     for m in range(NEAR // 2):
-        k2 = here_ref[m, :, :SLOTS].reshape(ROWS, D)
-        v2 = here_ref[m, :, SLOTS : 2 * SLOTS].reshape(ROWS, D)
+        k2 = near_ref[m, :, :SLOTS].reshape(ROWS, D)
+        v2 = near_ref[m, :, SLOTS : 2 * SLOTS].reshape(ROWS, D)
         got = dot(pick, jnp.concatenate([k2, v2], axis=1)).astype(BF16)
         far_ref[0, m * 32 : (m + 1) * 32] = got[:, :D]
         far_ref[1, m * 32 : (m + 1) * 32] = got[:, D:]
+        q = near_ref[m, :, 2 * SLOTS :].reshape(HEADS * 16, D)
+        q3_ref[m * 32 : (m + 1) * 32] = dot(pick16, q).astype(BF16)
 
 
 def two_parts(q):
@@ -123,7 +128,9 @@
     return peak, a * total_a + b * total_b, a * part_a + b * part_b
 
 
-def two_levels(qkv_ref, here_ref, there_ref, o_ref, lse_ref, k1, v1, k2, v2, s_scr, top_scr, first):
+def two_levels(qkv_ref, here_ref, there_hbm, o_ref, lse_ref, k1, v1, k2, v2, s_scr, top_scr, first, there_ref, sem):
+    fetch = pltpu.make_async_copy(there_hbm, there_ref, sem)
+    fetch.start()
     half = NEAR // 2
     for s in range(HEADS):
         rows = slice(s * ROWS, (s + 1) * ROWS)
@@ -155,6 +162,7 @@
             lse_ref[...] = (top + jnp.log2(total)).reshape(HEADS, SLOTS, D)[:, :8]
 
     scores(0)
+    fetch.wait()
     for i, ref in enumerate((here_ref, there_ref)):
         for m in range(half):
             at = (i * half + m) * ROWS
@@ -181,12 +189,11 @@
 
 def third_level(core_ref, here_ref, there_ref, far_a, far_b, third_ref):
     half = NEAR // 2
-    n = half * HEADS * 16
-    a = lax.broadcasted_iota(jnp.int32, (n // 2, n), 0)
-    b = lax.broadcasted_iota(jnp.int32, (n // 2, n), 1)
-    pick = jnp.where(b == ((a >> 3) << 4) + (a & 3), 1.0, 0.0).astype(BF16)
-    q3 = [dot(pick, ref[:, :, 2 * SLOTS :].reshape(n, D)) for ref in (here_ref, there_ref)]
-    q3 = jnp.concatenate(q3, axis=0)
+    n = half * HEADS * FAR
+    a = lax.broadcasted_iota(jnp.int32, (2 * n, n), 0)
+    b = lax.broadcasted_iota(jnp.int32, (2 * n, n), 1)
+    pick = jnp.where(b == ((a >> 3) << 2) + (a & 3), 1.0, 0.0).astype(BF16)
+    q3 = jnp.concatenate([dot(pick, here_ref[...]), dot(pick, there_ref[...])], axis=0).astype(BF16)
     k3 = jnp.concatenate([far_a[0], far_b[0]], axis=0)
     v3 = jnp.concatenate([far_a[1], far_b[1]], axis=0)
     level3 = attend(two_parts(q3), twice(k3), with_ones(v3))
@@ -253,7 +260,6 @@
     near = near.reshape(half * HEADS, 80, D)
     here = lax.all_to_all(near, ("outer", "inner"), 0, 0, tiled=True, axis_index_groups=same_core)
     here = here.reshape(half, HEADS, 80, D)
-    there = lax.ppermute(here, "outer", [(i, i ^ 1) for i in range(outer)])
     qkv = call(
         split_heads,
         [((HEADS, 3, ROWS, D), BF16)],
@@ -265,26 +271,35 @@
         limit=60 << 20,
     )
     qkv = lax.all_to_all(qkv, "inner", 0, 0, tiled=True)
-    far = call(pick_far, [((2, half * 32, D), BF16)], (here,))
+    far, q3_here, here = call(
+        pick_chosen,
+        [((2, half * 32, D), BF16), ((half * 32, D), BF16), ((half, HEADS, 2 * SLOTS, D), BF16)],
+        (here,),
+    )
+    other_core = [(i, i ^ 1) for i in range(outer)]
     place = [(g, j) for g in range(groups) for j in range(NEAR)]
     far_a, far_b = [
-        lax.ppermute(far, "outer", [(g * NEAR + j, (g + j // 2 + by) % groups * NEAR + j) for g, j in place])
-        for by in (0, groups // 2)
+        lax.ppermute(far, "outer", [(g * NEAR + j, (g + by[j // 2]) % groups * NEAR + j) for g, j in place])
+        for by in ((4, 1, 2, 3), (0, 5, 6, 7))
     ]
+    q3_there = lax.ppermute(q3_here, "outer", other_core)
+    there = lax.ppermute(here, "outer", other_core)
     third = call(
         third_level,
         [((NEAR, HEADS, 8, D), F32)],
-        (core, here, there, far_a, far_b),
+        (core, q3_here, q3_there, far_a, far_b),
         in_specs=[pl.BlockSpec(memory_space=pltpu.SMEM)] + vmem(4),
-        flops=1 << 28,
+        flops=1 << 32,
     )
     third = lax.all_to_all(third, "outer", 0, 0, tiled=True, axis_index_groups=near_groups)
     o, lse = call(
         two_levels,
         [((HEADS, ROWS, D), BF16), ((HEADS, 8, D), F32)],
         (qkv, here, there),
+        in_specs=vmem(2) + [anywhere],
         scratch=[pltpu.VMEM((HEADS * ROWS, 2 * D), BF16)] * 4
-        + [pltpu.VMEM((2, ROWS, HEADS * ROWS), F32), pltpu.VMEM((2, ROWS, D), F32), pltpu.VMEM((3, ROWS, D), F32)],
+        + [pltpu.VMEM((2, ROWS, HEADS * ROWS), F32), pltpu.VMEM((2, ROWS, D), F32), pltpu.VMEM((3, ROWS, D), F32)]
+        + [pltpu.VMEM((half, HEADS, 2 * SLOTS, D), BF16), pltpu.SemaphoreType.DMA],
         flops=1 << 33,
     )
     o = call(

time: 82.9 us -> 78 us (0.941)
  waiting for transfers between devices: 10.2 us -> 8.11 us
  starting transfers between devices: 42.1 us -> 40.4 us
  local copies, waits for them, and re-layouts: 1.09 us -> 0 us
    all_to_all x1, starting transfers between devices: 9.04 us -> 5.11 us  [body(): lax.all_to_all(third, 'outer', 0, 0, tiled=True, axis_index_groups=near_g...]
    ppermute x3 -> x4, waiting for transfers between devices: 2.53 us -> 0.01 us  [the longest x2 0.01 us: body(): lax.ppermute(far, 'outer', [(g * NEAR + j, (g + by[j // 2]) % groups * NE...]
    ppermute x3 -> x4, starting transfers between devices: 20.3 us -> 22.5 us  [the longest x2 15.7 us: body(): lax.ppermute(far, 'outer', [(g * NEAR + j, (g + by[j // 2]) % groups * NE...]
    unnamed x4 -> x0, local copies, waits for them, and re-layouts: 1.09 us -> none
  transfers between devices with their start and end apart: 6 -> 7, of which waited for: 2 -> 2; matrix products, arithmetic and copies ran while one was open for 0% -> 0% of each run, Pallas kernels for 12% -> 14%
where the time goes in v4:
time: 78 us; the launch traced here: 76.6 us
  starting transfers between devices  40.4 us (52%)
  Pallas kernels  14.5 us (19%)
  blocking collectives  13.5 us (17%)
  waiting for transfers between devices  8.11 us (10%)
    ppermute x2, starting transfers between devices, body(): lax.ppermute(far, 'outer', [(g * NEAR + j, (g + by[j // 2]) % groups * NE...  15.7 us
    pallas_call x7, Pallas kernels, call(): pl.pallas_call(kernel, out_shape=shapes, in_specs=in_specs or vmem(len(in...  14.5 us
    all_to_all x1, blocking collectives, body(): o = lax.all_to_all(o, 'inner', 0, 0, tiled=True)  13.5 us
    all_to_all x1, starting transfers between devices, body(): lax.all_to_all(near, ('outer', 'inner'), 0, 0, tiled=True, axis_index_gro...  9.24 us
    all_to_all x1, waiting for transfers between devices, body(): lax.all_to_all(near, ('outer', 'inner'), 0, 0, tiled=True, axis_index_gro...  7.69 us
    all_to_all x1, starting transfers between devices, body(): lax.all_to_all(third, 'outer', 0, 0, tiled=True, axis_index_groups=near_g...  5.11 us
    ppermute x1, starting transfers between devices, body(): q3_there = lax.ppermute(q3_here, 'outer', other_core)  4.91 us
    all_to_all x1, starting transfers between devices, body(): qkv = lax.all_to_all(qkv, 'inner', 0, 0, tiled=True)  3.58 us
  transfers between devices with their start and end apart: 7, of which 2 were waited for; matrix products, arithmetic and copies ran while one was open for 0% of the time, Pallas kernels for 14%

profile of v4, /device:TPU:1, one launch (start us, length us, event | category | flops | bytes accessed | tf_op | source)
XLA Modules:
  0.0 76.6 jit_solution(8383640801595228281)
XLA Ops:
  0.0 2.6 %shard_map.38 = bf16[4,8,80,128]{3,2,1,0:T(8,128)(2,1)} custom-call(bf16[256,1024]{1,0:T(8,128)(2,1)} %q_hbm.3, bf16[256,1024]{1,0:T(8,128)(2,1)} %k_hbm.3, bf16[256,1024]{1,0:T(8,128)(2,1)} %v_hbm.3), custom_call_target="tpu_custom_call" | custom-call | bytes 1048576 | tf_op jit(solution)/shard_map/pallas_call | solution.py:220
  2.6 9.2 %all-to-all-start.1 = ((bf16[32,80,128]{2,1,0:T(8,128)(2,1)}), bf16[32,80,128]{2,1,0:T(8,128)(2,1)S(1)}, u32[]{:S(2)}, u32[]{:S(2)}) async-start(bf16[32,80,128]{2,1,0:T(8,128)(2,1)} %bitcast.4), calls=%async_computation.1 | async-start | bytes 1310720 | tf_op jit(solution)/shard_map/all_to_all | solution.py:261
  11.9 2.9 %shard_map.37 = bf16[8,3,256,128]{3,2,1,0:T(8,128)(2,1)} custom-call(bf16[256,1024]{1,0:T(8,128)(2,1)} %q_hbm.3, bf16[256,1024]{1,0:T(8,128)(2,1)} %k_hbm.3, bf16[256,1024]{1,0:T(8,128)(2,1)} %v_hbm.3), custom_call_target="tpu_custom_call" | custom-call | bytes 1048576 | tf_op jit(solution)/shard_map/pallas_call | solution.py:220
  14.8 7.7 %all-to-all-done.1 = bf16[32,80,128]{2,1,0:T(8,128)(2,1)S(1)} async-done(((bf16[32,80,128]{2,1,0:T(8,128)(2,1)}), bf16[32,80,128]{2,1,0:T(8,128)(2,1)S(1)}, u32[]{:S(2)}, u32[]{:S(2)}) %all-to-all-start.1) | async-done | bytes 655392 | tf_op jit(solution)/shard_map/all_to_all | solution.py:261
  22.5 3.6 %all-to-all-start = ((bf16[8,3,256,128]{3,2,1,0:T(8,128)(2,1)}), bf16[8,3,256,128]{3,2,1,0:T(8,128)(2,1)S(1)}, u32[]{:S(2)}, u32[]{:S(2)}) async-start(bf16[8,3,256,128]{3,2,1,0:T(8,128)(2,1)} %shard_map.37), calls=%async_computation | async-start | bytes 3145728 | tf_op jit(solution)/shard_map/all_to_all | solution.py:273
  26.1 0.2 shard_map.39
  26.3 15.0 %collective-permute-start.2 = (bf16[2,128,128]{2,1,0:T(8,128)(2,1)S(1)}, bf16[2,128,128]{2,1,0:T(8,128)(2,1)S(1)}, u32[]{:S(2)}, u32[]{:S(2)}) collective-permute-start(bf16[2,128,128]{2,1,0:T(8,128)(2,1)S(1)} %get-tuple-element.13), channel_id=1, source_target_pairs={{0,256},{8,264},{16,80},{24,88},{32,160},{40,168},{48,240},{56,248... | collective-permute-start | bytes 196616 | tf_op jit(solution)/shard_map/ppermute | solution.py:282
  41.3 0.7 collective-permute-start.3
  42.0 4.9 %collective-permute-start.1 = (bf16[128,128]{1,0:T(8,128)(2,1)S(1)}, bf16[128,128]{1,0:T(8,128)(2,1)S(1)}, u32[]{:S(2)}, u32[]{:S(2)}) collective-permute-start(bf16[128,128]{1,0:T(8,128)(2,1)S(1)} %get-tuple-element.12.here_ref), channel_id=1, source_target_pairs={{0,8},{8,0},{16,24},{24,16},{32,40},{40,32},{48,56},{56,48},{64,72... | collective-permute-start | bytes 98312 | tf_op jit(solution)/shard_map/ppermute | solution.py:285
  46.9 1.9 %collective-permute-start = (bf16[4,8,64,128]{3,2,1,0:T(8,128)(2,1)S(1)}, bf16[4,8,64,128]{3,2,1,0:T(8,128)(2,1)S(1)}, u32[]{:S(2)}, u32[]{:S(2)}) collective-permute-start(bf16[4,8,64,128]{3,2,1,0:T(8,128)(2,1)S(1)} %get-tuple-element.10.here_ref), channel_id=1, source_target_pairs={{0,8},{8,0},{16,24},{24,16},{32,40},{40,32},{48,56},{56,48},{64,72... | collective-permute-start | bytes 1572872 | tf_op jit(solution)/shard_map/ppermute | solution.py:286
  48.9 0.0 collective-permute-done.1.there_ref
  48.9 0.0 collective-permute-done.2.far_a
  48.9 0.0 collective-permute-done.3.far_b
  48.9 1.3 %shard_map.41 = f32[8,8,8,128]{3,2,1,0:T(8,128)} custom-call(s32[1]{0:T(128)} %bitcast.2.core_ref, bf16[128,128]{1,0:T(8,128)(2,1)S(1)} %get-tuple-element.12.here_ref, bf16[128,128]{1,0:T(8,128)(2,1)S(1)} %collective-permute-done.1.there_ref, bf16[2,128,128]{2,1,0:T(8,128)(2,1)S(1)} %collective-permute-done.2.far_a, ...), custom_call_target="tpu_custom_call" | custom-call | flops 4294967296 | bytes 1048576 | tf_op jit(solution)/shard_map/pallas_call | solution.py:220
  50.2 0.0 all-to-all-done.qkv_ref
  50.2 5.1 %all-to-all-start.2 = ((f32[8,8,8,128]{3,2,1,0:T(8,128)}), f32[8,8,8,128]{3,2,1,0:T(8,128)S(1)}, u32[]{:S(2)}, u32[]{:S(2)}) async-start(f32[8,8,8,128]{3,2,1,0:T(8,128)} %shard_map.41), calls=%async_computation.2 | async-start | bytes 524288 | tf_op jit(solution)/shard_map/all_to_all | solution.py:294
  55.3 0.0 collective-permute-done.there_hbm
  55.3 6.0 %shard_map.40 = (bf16[8,256,128]{2,1,0:T(8,128)(2,1)S(1)}, f32[8,8,128]{2,1,0:T(8,128)S(1)}) custom-call(bf16[8,3,256,128]{3,2,1,0:T(8,128)(2,1)S(1)} %all-to-all-done.qkv_ref, bf16[4,8,64,128]{3,2,1,0:T(8,128)(2,1)S(1)} %get-tuple-element.10.here_ref, bf16[4,8,64,128]{3,2,1,0:T(8,128)(2,1)S(1)} %collective-permute-done.there_hbm), custom_call_target="tpu_custom_call" | custom-call | flops 8589934592 | bytes 1048576 | tf_op jit(solution)/shard_map/pallas_call | solution.py:220
  61.3 0.4 all-to-all-done.2.third_ref
  61.7 0.1 shard_map.42
  61.9 13.5 %all_to_all.20.o_ref = bf16[8,256,128]{2,1,0:T(8,128)(2,1)S(1)} all-to-all(bf16[8,256,128]{2,1,0:T(8,128)(2,1)S(1)} %shard_map.42), channel_id=1, replica_groups=mesh['outer'=64,'inner'=8] {'inner'}, dimensions={0} | all-to-all | bytes 1048576 | tf_op jit(solution)/shard_map/all_to_all | solution.py:314
  75.3 1.3 %shard_map.43 = bf16[256,1024]{1,0:T(8,128)(2,1)} custom-call(bf16[8,256,128]{2,1,0:T(8,128)(2,1)S(1)} %all_to_all.20.o_ref), custom_call_target="tpu_custom_call" | custom-call | bytes 1048576 | tf_op jit(solution)/shard_map/pallas_call | solution.py:220
Async XLA Ops:
  2.6 19.9 %all-to-all-start.1 = ((bf16[32,80,128]{2,1,0:T(8,128)(2,1)}), bf16[32,80,128]{2,1,0:T(8,128)(2,1)S(1)}, u32[]{:S(2)}, u32[]{:S(2)}) async-start(bf16[32,80,128]{2,1,0:T(8,128)(2,1)} %bitcast.4), calls=%async_computation.1 | async-start | bytes 1310720 | tf_op jit(solution)/shard_map/all_to_all | solution.py:261
  22.5 27.7 %all-to-all-start = ((bf16[8,3,256,128]{3,2,1,0:T(8,128)(2,1)}), bf16[8,3,256,128]{3,2,1,0:T(8,128)(2,1)S(1)}, u32[]{:S(2)}, u32[]{:S(2)}) async-start(bf16[8,3,256,128]{3,2,1,0:T(8,128)(2,1)} %shard_map.37), calls=%async_computation | async-start | bytes 3145728 | tf_op jit(solution)/shard_map/all_to_all | solution.py:273
  26.3 22.5 %collective-permute-start.2 = (bf16[2,128,128]{2,1,0:T(8,128)(2,1)S(1)}, bf16[2,128,128]{2,1,0:T(8,128)(2,1)S(1)}, u32[]{:S(2)}, u32[]{:S(2)}) collective-permute-start(bf16[2,128,128]{2,1,0:T(8,128)(2,1)S(1)} %get-tuple-element.13), channel_id=1, source_target_pairs={{0,256},{8,264},{16,80},{24,88},{32,160},{40,168},{48,240},{56,248... | collective-permute-start | bytes 196616 | tf_op jit(solution)/shard_map/ppermute | solution.py:282
  41.3 7.5 %collective-permute-start.3 = (bf16[2,128,128]{2,1,0:T(8,128)(2,1)S(1)}, bf16[2,128,128]{2,1,0:T(8,128)(2,1)S(1)}, u32[]{:S(2)}, u32[]{:S(2)}) collective-permute-start(bf16[2,128,128]{2,1,0:T(8,128)(2,1)S(1)} %get-tuple-element.13), channel_id=1, source_target_pairs={{0,0},{8,8},{16,336},{24,344},{32,416},{40,424},{48,496},{56,504},... | collective-permute-start | bytes 196616 | tf_op jit(solution)/shard_map/ppermute | solution.py:282
  42.0 6.9 %collective-permute-start.1 = (bf16[128,128]{1,0:T(8,128)(2,1)S(1)}, bf16[128,128]{1,0:T(8,128)(2,1)S(1)}, u32[]{:S(2)}, u32[]{:S(2)}) collective-permute-start(bf16[128,128]{1,0:T(8,128)(2,1)S(1)} %get-tuple-element.12.here_ref), channel_id=1, source_target_pairs={{0,8},{8,0},{16,24},{24,16},{32,40},{40,32},{48,56},{56,48},{64,72... | collective-permute-start | bytes 98312 | tf_op jit(solution)/shard_map/ppermute | solution.py:285
  46.9 8.4 %collective-permute-start = (bf16[4,8,64,128]{3,2,1,0:T(8,128)(2,1)S(1)}, bf16[4,8,64,128]{3,2,1,0:T(8,128)(2,1)S(1)}, u32[]{:S(2)}, u32[]{:S(2)}) collective-permute-start(bf16[4,8,64,128]{3,2,1,0:T(8,128)(2,1)S(1)} %get-tuple-element.10.here_ref), channel_id=1, source_target_pairs={{0,8},{8,0},{16,24},{24,16},{32,40},{40,32},{48,56},{56,48},{64,72... | collective-permute-start | bytes 1572872 | tf_op jit(solution)/shard_map/ppermute | solution.py:286
  50.2 11.5 %all-to-all-start.2 = ((f32[8,8,8,128]{3,2,1,0:T(8,128)}), f32[8,8,8,128]{3,2,1,0:T(8,128)S(1)}, u32[]{:S(2)}, u32[]{:S(2)}) async-start(f32[8,8,8,128]{3,2,1,0:T(8,128)} %shard_map.41), calls=%async_computation.2 | async-start | bytes 524288 | tf_op jit(solution)/shard_map/all_to_all | solution.py:294

commit v5 on v4

--- a/solution.py
+++ b/solution.py
@@ -44,21 +44,39 @@
     return jnp.dot(a, b, preferred_element_type=F32)
 
 
-def chosen_rows(q_hbm, k_hbm, v_hbm, near_ref, q_scr, k_scr, v_scr, sems):
-    pairs = ((k_hbm, k_scr), (v_hbm, v_scr), (q_hbm, q_scr))
-    copies = [pltpu.make_async_copy(src, dst, sems.at[i]) for i, (src, dst) in enumerate(pairs)]
+def chosen_rows(q_hbm, k_hbm, v_hbm, near_hbm, q_scr, k_scr, v_scr, out_scr, in_sems, out_sems):
+    copies = [pltpu.make_async_copy(k_hbm, k_scr, in_sems.at[0]), pltpu.make_async_copy(v_hbm, v_scr, in_sems.at[1])]
+    copies += [
+        pltpu.make_async_copy(q_hbm.at[pl.ds(64 * s, 8)], q_scr.at[pl.ds(8 * s, 8)], in_sems.at[2 + s])
+        for s in range(FAR)
+    ]
     for c in copies:
         c.start()
-    for c in copies:
-        c.wait()
+    written = []
+
+    def send(i, at, rows):
+        part = (slice(None), pl.ds(at, rows))
+        for m in range(NEAR // 2):
+            c = pltpu.make_async_copy(out_scr.at[part], near_hbm.at[(m, *part)], out_sems.at[i, m])
+            c.start()
+            written.append(c)
+
+    for i, scr in enumerate((k_scr, v_scr)):
+        copies[i].wait()
+        for h in range(HEADS):
+            got = dot(to_order(h, SLOTS), scr[:, h * D : (h + 1) * D])
+            out_scr[h, i * SLOTS : (i + 1) * SLOTS] = got.astype(BF16)
+        send(i, i * SLOTS, SLOTS)
+    for c in copies[2:]:
+        c.wait()
+    slot = lax.broadcasted_iota(jnp.int32, (16, 8 * FAR), 0)
+    row = lax.broadcasted_iota(jnp.int32, (16, 8 * FAR), 1)
     for h in range(HEADS):
-        cols = slice(h * D, (h + 1) * D)
-        rows = jnp.concatenate([k_scr[:, cols], v_scr[:, cols], q_scr[:, cols]], axis=1)
-        out = dot(to_order(h, SLOTS), rows).astype(BF16)
-        for m in range(NEAR // 2):
-            near_ref[m, h, :SLOTS] = out[:, :D]
-            near_ref[m, h, SLOTS : 2 * SLOTS] = out[:, D : 2 * D]
-            near_ref[m, h, 2 * SLOTS :] = out[:16, 2 * D :]
+        pick = jnp.where((row == 8 * slot + h) & (slot < FAR), 1.0, 0.0).astype(BF16)
+        out_scr[h, 2 * SLOTS :] = dot(pick, q_scr[:, h * D : (h + 1) * D]).astype(BF16)
+    send(2, 2 * SLOTS, 16)
+    for c in written:
+        c.wait()
 
 
 def split_heads(q_hbm, k_hbm, v_hbm, qkv_hbm, q_scr, k_scr, v_scr, out_scr, in_sems, out_sems):
@@ -187,7 +205,7 @@
     o_ref[...] = jnp.concatenate([last, o[:, 8:]], axis=1).astype(BF16)
 
 
-def third_level(core_ref, here_ref, there_ref, far_a, far_b, third_ref):
+def third_level(core_ref, here_ref, there_ref, far_a, far_b, third_hbm, third_scr, sems):
     half = NEAR // 2
     n = half * HEADS * FAR
     a = lax.broadcasted_iota(jnp.int32, (2 * n, n), 0)
@@ -199,15 +217,30 @@
     level3 = attend(two_parts(q3), twice(k3), with_ones(v3))
     row = lax.broadcasted_iota(jnp.int32, (HEADS * 8, D), 0) & 7
     core = core_ref[0]
+    written = []
     for j in range(NEAR):
         t, l, o = [x[j * 64 : (j + 1) * 64] for x in level3]
         at = 2 * j + core if j < half else 2 * (j - half) + 1 - core
-        third_ref[at] = jnp.where(row < 4, o / l, t + jnp.log2(l)).reshape(HEADS, 8, D)
-
-
-def finish(o_ref, out_ref):
-    for h in range(HEADS):
-        out_ref[:, h * D : (h + 1) * D] = dot(from_order(h), o_ref[h]).astype(BF16)
+        third_scr[j] = jnp.where(row < 4, o / l, t + jnp.log2(l)).reshape(HEADS, 8, D)
+        c = pltpu.make_async_copy(third_scr.at[j], third_hbm.at[at], sems.at[j])
+        c.start()
+        written.append(c)
+    for c in written:
+        c.wait()
+
+
+def finish(o_ref, out_hbm, out_scr, sems):
+    orders = [from_order(h) for h in range(HEADS)]
+    written = []
+    for i in range(4):
+        rows = slice(i * ROWS // 4, (i + 1) * ROWS // 4)
+        for h in range(HEADS):
+            out_scr[rows, h * D : (h + 1) * D] = dot(orders[h][rows], o_ref[h]).astype(BF16)
+        c = pltpu.make_async_copy(out_scr.at[rows], out_hbm.at[rows], sems.at[i])
+        c.start()
+        written.append(c)
+    for c in written:
+        c.wait()
 
 
 def vmem(n):
@@ -254,7 +287,15 @@
         [((half, HEADS, 80, D), BF16)],
         (queries, keys, values),
         in_specs=[anywhere] * 3,
-        scratch=[block] * 3 + [pltpu.SemaphoreType.DMA((3,))],
+        out_specs=[anywhere],
+        scratch=[
+            pltpu.VMEM((8 * FAR, HEADS * D), BF16),
+            block,
+            block,
+            pltpu.VMEM((HEADS, 80, D), BF16),
+            pltpu.SemaphoreType.DMA((2 + FAR,)),
+            pltpu.SemaphoreType.DMA((3, half)),
+        ],
         limit=60 << 20,
     )
     near = near.reshape(half * HEADS, 80, D)
@@ -289,6 +330,8 @@
         [((NEAR, HEADS, 8, D), F32)],
         (core, q3_here, q3_there, far_a, far_b),
         in_specs=[pl.BlockSpec(memory_space=pltpu.SMEM)] + vmem(4),
+        out_specs=[anywhere],
+        scratch=[pltpu.VMEM((NEAR, HEADS, 8, D), F32), pltpu.SemaphoreType.DMA((NEAR,))],
         flops=1 << 32,
     )
     third = lax.all_to_all(third, "outer", 0, 0, tiled=True, axis_index_groups=near_groups)
@@ -312,7 +355,13 @@
         aliases={2: 0},
     )
     o = lax.all_to_all(o, "inner", 0, 0, tiled=True)
-    return call(finish, [((ROWS, HEADS * D), BF16)], (o,))
+    return call(
+        finish,
+        [((ROWS, HEADS * D), BF16)],
+        (o,),
+        out_specs=[anywhere],
+        scratch=[block, pltpu.SemaphoreType.DMA((4,))],
+    )
 
 
 def solution(mesh):

time: 78 us -> 77.7 us (level)
  no operation moved by 1% of the time
where the time goes in v5:
time: 77.7 us; the launch traced here: 76.3 us
  starting transfers between devices  40.4 us (52%)
  Pallas kernels  14.2 us (18%)
  blocking collectives  13.5 us (17%)
  waiting for transfers between devices  8.12 us (10%)
    ppermute x2, starting transfers between devices, body(): lax.ppermute(far, 'outer', [(g * NEAR + j, (g + by[j // 2]) % groups * NE...  15.7 us
    pallas_call x7, Pallas kernels, call(): pl.pallas_call(kernel, out_shape=shapes, in_specs=in_specs or vmem(len(in...  14.2 us
    all_to_all x1, blocking collectives, body(): o = lax.all_to_all(o, 'inner', 0, 0, tiled=True)  13.5 us
    all_to_all x1, starting transfers between devices, body(): lax.all_to_all(near, ('outer', 'inner'), 0, 0, tiled=True, axis_index_gro...  9.23 us
    all_to_all x1, waiting for transfers between devices, body(): lax.all_to_all(near, ('outer', 'inner'), 0, 0, tiled=True, axis_index_gro...  7.7 us
    all_to_all x1, starting transfers between devices, body(): lax.all_to_all(third, 'outer', 0, 0, tiled=True, axis_index_groups=near_g...  5.12 us
    ppermute x1, starting transfers between devices, body(): q3_there = lax.ppermute(q3_here, 'outer', other_core)  4.91 us
    all_to_all x1, starting transfers between devices, body(): qkv = lax.all_to_all(qkv, 'inner', 0, 0, tiled=True)  3.58 us
  transfers between devices with their start and end apart: 7, of which 2 were waited for; matrix products, arithmetic and copies ran while one was open for 0% of the time, Pallas kernels for 14%

profile of v5, /device:TPU:1, one launch (start us, length us, event | category | flops | bytes accessed | tf_op | source)
XLA Modules:
  0.0 76.3 jit_solution(5095002522049367464)
XLA Ops:
  0.0 2.4 %shard_map.38 = bf16[4,8,80,128]{3,2,1,0:T(8,128)(2,1)} custom-call(bf16[256,1024]{1,0:T(8,128)(2,1)} %q_hbm.3, bf16[256,1024]{1,0:T(8,128)(2,1)} %k_hbm.3, bf16[256,1024]{1,0:T(8,128)(2,1)} %v_hbm.3), custom_call_target="tpu_custom_call" | custom-call | bytes 1048576 | tf_op jit(solution)/shard_map/pallas_call | solution.py:253
  2.4 9.2 %all-to-all-start.1 = ((bf16[32,80,128]{2,1,0:T(8,128)(2,1)}), bf16[32,80,128]{2,1,0:T(8,128)(2,1)S(1)}, u32[]{:S(2)}, u32[]{:S(2)}) async-start(bf16[32,80,128]{2,1,0:T(8,128)(2,1)} %bitcast.4), calls=%async_computation.1 | async-start | bytes 1310720 | tf_op jit(solution)/shard_map/all_to_all | solution.py:302
  11.7 2.9 %shard_map.37 = bf16[8,3,256,128]{3,2,1,0:T(8,128)(2,1)} custom-call(bf16[256,1024]{1,0:T(8,128)(2,1)} %q_hbm.3, bf16[256,1024]{1,0:T(8,128)(2,1)} %k_hbm.3, bf16[256,1024]{1,0:T(8,128)(2,1)} %v_hbm.3), custom_call_target="tpu_custom_call" | custom-call | bytes 1048576 | tf_op jit(solution)/shard_map/pallas_call | solution.py:253
  14.6 7.7 %all-to-all-done.1 = bf16[32,80,128]{2,1,0:T(8,128)(2,1)S(1)} async-done(((bf16[32,80,128]{2,1,0:T(8,128)(2,1)}), bf16[32,80,128]{2,1,0:T(8,128)(2,1)S(1)}, u32[]{:S(2)}, u32[]{:S(2)}) %all-to-all-start.1) | async-done | bytes 655392 | tf_op jit(solution)/shard_map/all_to_all | solution.py:302
  22.3 3.6 %all-to-all-start = ((bf16[8,3,256,128]{3,2,1,0:T(8,128)(2,1)}), bf16[8,3,256,128]{3,2,1,0:T(8,128)(2,1)S(1)}, u32[]{:S(2)}, u32[]{:S(2)}) async-start(bf16[8,3,256,128]{3,2,1,0:T(8,128)(2,1)} %shard_map.37), calls=%async_computation | async-start | bytes 3145728 | tf_op jit(solution)/shard_map/all_to_all | solution.py:314
  25.9 0.2 shard_map.39
  26.2 15.0 %collective-permute-start.2 = (bf16[2,128,128]{2,1,0:T(8,128)(2,1)S(1)}, bf16[2,128,128]{2,1,0:T(8,128)(2,1)S(1)}, u32[]{:S(2)}, u32[]{:S(2)}) collective-permute-start(bf16[2,128,128]{2,1,0:T(8,128)(2,1)S(1)} %get-tuple-element.13), channel_id=1, source_target_pairs={{0,256},{8,264},{16,80},{24,88},{32,160},{40,168},{48,240},{56,248... | collective-permute-start | bytes 196616 | tf_op jit(solution)/shard_map/ppermute | solution.py:323
  41.2 0.7 collective-permute-start.3
  41.8 4.9 %collective-permute-start.1 = (bf16[128,128]{1,0:T(8,128)(2,1)S(1)}, bf16[128,128]{1,0:T(8,128)(2,1)S(1)}, u32[]{:S(2)}, u32[]{:S(2)}) collective-permute-start(bf16[128,128]{1,0:T(8,128)(2,1)S(1)} %get-tuple-element.12.here_ref), channel_id=1, source_target_pairs={{0,8},{8,0},{16,24},{24,16},{32,40},{40,32},{48,56},{56,48},{64,72... | collective-permute-start | bytes 98312 | tf_op jit(solution)/shard_map/ppermute | solution.py:326
  46.7 1.9 %collective-permute-start = (bf16[4,8,64,128]{3,2,1,0:T(8,128)(2,1)S(1)}, bf16[4,8,64,128]{3,2,1,0:T(8,128)(2,1)S(1)}, u32[]{:S(2)}, u32[]{:S(2)}) collective-permute-start(bf16[4,8,64,128]{3,2,1,0:T(8,128)(2,1)S(1)} %get-tuple-element.10.here_ref), channel_id=1, source_target_pairs={{0,8},{8,0},{16,24},{24,16},{32,40},{40,32},{48,56},{56,48},{64,72... | collective-permute-start | bytes 1572872 | tf_op jit(solution)/shard_map/ppermute | solution.py:327
  48.7 0.0 collective-permute-done.1.there_ref
  48.7 0.0 collective-permute-done.2.far_a
  48.7 0.0 collective-permute-done.3.far_b
  48.7 1.3 %shard_map.41 = f32[8,8,8,128]{3,2,1,0:T(8,128)} custom-call(s32[1]{0:T(128)} %bitcast.2.core_ref, bf16[128,128]{1,0:T(8,128)(2,1)S(1)} %get-tuple-element.12.here_ref, bf16[128,128]{1,0:T(8,128)(2,1)S(1)} %collective-permute-done.1.there_ref, bf16[2,128,128]{2,1,0:T(8,128)(2,1)S(1)} %collective-permute-done.2.far_a, ...), custom_call_target="tpu_custom_call" | custom-call | flops 4294967296 | bytes 1048576 | tf_op jit(solution)/shard_map/pallas_call | solution.py:253
  50.0 0.0 all-to-all-done.qkv_ref
  50.0 5.1 %all-to-all-start.2 = ((f32[8,8,8,128]{3,2,1,0:T(8,128)}), f32[8,8,8,128]{3,2,1,0:T(8,128)S(1)}, u32[]{:S(2)}, u32[]{:S(2)}) async-start(f32[8,8,8,128]{3,2,1,0:T(8,128)} %shard_map.41), calls=%async_computation.2 | async-start | bytes 524288 | tf_op jit(solution)/shard_map/all_to_all | solution.py:337
  55.1 0.0 collective-permute-done.there_hbm
  55.1 6.0 %shard_map.40 = (bf16[8,256,128]{2,1,0:T(8,128)(2,1)S(1)}, f32[8,8,128]{2,1,0:T(8,128)S(1)}) custom-call(bf16[8,3,256,128]{3,2,1,0:T(8,128)(2,1)S(1)} %all-to-all-done.qkv_ref, bf16[4,8,64,128]{3,2,1,0:T(8,128)(2,1)S(1)} %get-tuple-element.10.here_ref, bf16[4,8,64,128]{3,2,1,0:T(8,128)(2,1)S(1)} %collective-permute-done.there_hbm), custom_call_target="tpu_custom_call" | custom-call | flops 8589934592 | bytes 1048576 | tf_op jit(solution)/shard_map/pallas_call | solution.py:253
  61.2 0.4 all-to-all-done.2.third_ref
  61.6 0.1 shard_map.42
  61.7 13.5 %all_to_all.20.o_ref = bf16[8,256,128]{2,1,0:T(8,128)(2,1)S(1)} all-to-all(bf16[8,256,128]{2,1,0:T(8,128)(2,1)S(1)} %shard_map.42), channel_id=1, replica_groups=mesh['outer'=64,'inner'=8] {'inner'}, dimensions={0} | all-to-all | bytes 1048576 | tf_op jit(solution)/shard_map/all_to_all | solution.py:357
  75.1 1.2 %shard_map.43 = bf16[256,1024]{1,0:T(8,128)(2,1)} custom-call(bf16[8,256,128]{2,1,0:T(8,128)(2,1)S(1)} %all_to_all.20.o_ref), custom_call_target="tpu_custom_call" | custom-call | bytes 1048576 | tf_op jit(solution)/shard_map/pallas_call | solution.py:253
Async XLA Ops:
  2.4 19.9 %all-to-all-start.1 = ((bf16[32,80,128]{2,1,0:T(8,128)(2,1)}), bf16[32,80,128]{2,1,0:T(8,128)(2,1)S(1)}, u32[]{:S(2)}, u32[]{:S(2)}) async-start(bf16[32,80,128]{2,1,0:T(8,128)(2,1)} %bitcast.4), calls=%async_computation.1 | async-start | bytes 1310720 | tf_op jit(solution)/shard_map/all_to_all | solution.py:302
  22.3 27.7 %all-to-all-start = ((bf16[8,3,256,128]{3,2,1,0:T(8,128)(2,1)}), bf16[8,3,256,128]{3,2,1,0:T(8,128)(2,1)S(1)}, u32[]{:S(2)}, u32[]{:S(2)}) async-start(bf16[8,3,256,128]{3,2,1,0:T(8,128)(2,1)} %shard_map.37), calls=%async_computation | async-start | bytes 3145728 | tf_op jit(solution)/shard_map/all_to_all | solution.py:314
  26.2 22.5 %collective-permute-start.2 = (bf16[2,128,128]{2,1,0:T(8,128)(2,1)S(1)}, bf16[2,128,128]{2,1,0:T(8,128)(2,1)S(1)}, u32[]{:S(2)}, u32[]{:S(2)}) collective-permute-start(bf16[2,128,128]{2,1,0:T(8,128)(2,1)S(1)} %get-tuple-element.13), channel_id=1, source_target_pairs={{0,256},{8,264},{16,80},{24,88},{32,160},{40,168},{48,240},{56,248... | collective-permute-start | bytes 196616 | tf_op jit(solution)/shard_map/ppermute | solution.py:323
  41.2 7.5 %collective-permute-start.3 = (bf16[2,128,128]{2,1,0:T(8,128)(2,1)S(1)}, bf16[2,128,128]{2,1,0:T(8,128)(2,1)S(1)}, u32[]{:S(2)}, u32[]{:S(2)}) collective-permute-start(bf16[2,128,128]{2,1,0:T(8,128)(2,1)S(1)} %get-tuple-element.13), channel_id=1, source_target_pairs={{0,0},{8,8},{16,336},{24,344},{32,416},{40,424},{48,496},{56,504},... | collective-permute-start | bytes 196616 | tf_op jit(solution)/shard_map/ppermute | solution.py:323
  41.8 6.9 %collective-permute-start.1 = (bf16[128,128]{1,0:T(8,128)(2,1)S(1)}, bf16[128,128]{1,0:T(8,128)(2,1)S(1)}, u32[]{:S(2)}, u32[]{:S(2)}) collective-permute-start(bf16[128,128]{1,0:T(8,128)(2,1)S(1)} %get-tuple-element.12.here_ref), channel_id=1, source_target_pairs={{0,8},{8,0},{16,24},{24,16},{32,40},{40,32},{48,56},{56,48},{64,72... | collective-permute-start | bytes 98312 | tf_op jit(solution)/shard_map/ppermute | solution.py:326
  46.7 8.4 %collective-permute-start = (bf16[4,8,64,128]{3,2,1,0:T(8,128)(2,1)S(1)}, bf16[4,8,64,128]{3,2,1,0:T(8,128)(2,1)S(1)}, u32[]{:S(2)}, u32[]{:S(2)}) collective-permute-start(bf16[4,8,64,128]{3,2,1,0:T(8,128)(2,1)S(1)} %get-tuple-element.10.here_ref), channel_id=1, source_target_pairs={{0,8},{8,0},{16,24},{24,16},{32,40},{40,32},{48,56},{56,48},{64,72... | collective-permute-start | bytes 1572872 | tf_op jit(solution)/shard_map/ppermute | solution.py:327
  50.0 11.5 %all-to-all-start.2 = ((f32[8,8,8,128]{3,2,1,0:T(8,128)}), f32[8,8,8,128]{3,2,1,0:T(8,128)S(1)}, u32[]{:S(2)}, u32[]{:S(2)}) async-start(f32[8,8,8,128]{3,2,1,0:T(8,128)} %shard_map.41), calls=%async_computation.2 | async-start | bytes 524288 | tf_op jit(solution)/shard_map/all_to_all | solution.py:337

commit v6 on v5

--- a/solution.py
+++ b/solution.py
@@ -47,7 +47,7 @@
 def chosen_rows(q_hbm, k_hbm, v_hbm, near_hbm, q_scr, k_scr, v_scr, out_scr, in_sems, out_sems):
     copies = [pltpu.make_async_copy(k_hbm, k_scr, in_sems.at[0]), pltpu.make_async_copy(v_hbm, v_scr, in_sems.at[1])]
     copies += [
-        pltpu.make_async_copy(q_hbm.at[pl.ds(64 * s, 8)], q_scr.at[pl.ds(8 * s, 8)], in_sems.at[2 + s])
+        pltpu.make_async_copy(q_hbm.at[pl.ds(64 * s, 16)], q_scr.at[pl.ds(16 * s, 16)], in_sems.at[2 + s])
         for s in range(FAR)
     ]
     for c in copies:
@@ -69,10 +69,10 @@
         send(i, i * SLOTS, SLOTS)
     for c in copies[2:]:
         c.wait()
-    slot = lax.broadcasted_iota(jnp.int32, (16, 8 * FAR), 0)
-    row = lax.broadcasted_iota(jnp.int32, (16, 8 * FAR), 1)
+    slot = lax.broadcasted_iota(jnp.int32, (16, 16 * FAR), 0)
+    row = lax.broadcasted_iota(jnp.int32, (16, 16 * FAR), 1)
     for h in range(HEADS):
-        pick = jnp.where((row == 8 * slot + h) & (slot < FAR), 1.0, 0.0).astype(BF16)
+        pick = jnp.where((row == 16 * slot + h) & (slot < FAR), 1.0, 0.0).astype(BF16)
         out_scr[h, 2 * SLOTS :] = dot(pick, q_scr[:, h * D : (h + 1) * D]).astype(BF16)
     send(2, 2 * SLOTS, 16)
     for c in written:
@@ -289,7 +289,7 @@
         in_specs=[anywhere] * 3,
         out_specs=[anywhere],
         scratch=[
-            pltpu.VMEM((8 * FAR, HEADS * D), BF16),
+            pltpu.VMEM((16 * FAR, HEADS * D), BF16),
             block,
             block,
             pltpu.VMEM((HEADS, 80, D), BF16),

time: 77.7 us -> 77.7 us (level)
  no operation moved by 1% of the time
where the time goes in v6:
time: 77.7 us; the launch traced here: 76.3 us
  starting transfers between devices  40.4 us (52%)
  Pallas kernels  14.2 us (18%)
  blocking collectives  13.5 us (17%)
  waiting for transfers between devices  8.12 us (10%)
    ppermute x2, starting transfers between devices, body(): lax.ppermute(far, 'outer', [(g * NEAR + j, (g + by[j // 2]) % groups * NE...  15.7 us
    pallas_call x7, Pallas kernels, call(): pl.pallas_call(kernel, out_shape=shapes, in_specs=in_specs or vmem(len(in...  14.2 us
    all_to_all x1, blocking collectives, body(): o = lax.all_to_all(o, 'inner', 0, 0, tiled=True)  13.5 us
    all_to_all x1, starting transfers between devices, body(): lax.all_to_all(near, ('outer', 'inner'), 0, 0, tiled=True, axis_index_gro...  9.23 us
    all_to_all x1, waiting for transfers between devices, body(): lax.all_to_all(near, ('outer', 'inner'), 0, 0, tiled=True, axis_index_gro...  7.7 us
    all_to_all x1, starting transfers between devices, body(): lax.all_to_all(third, 'outer', 0, 0, tiled=True, axis_index_groups=near_g...  5.12 us
    ppermute x1, starting transfers between devices, body(): q3_there = lax.ppermute(q3_here, 'outer', other_core)  4.91 us
    all_to_all x1, starting transfers between devices, body(): qkv = lax.all_to_all(qkv, 'inner', 0, 0, tiled=True)  3.58 us
  transfers between devices with their start and end apart: 7, of which 2 were waited for; matrix products, arithmetic and copies ran while one was open for 0% of the time, Pallas kernels for 14%

profile of v6, /device:TPU:1, one launch (start us, length us, event | category | flops | bytes accessed | tf_op | source)
XLA Modules:
  0.0 76.3 jit_solution(18322997946437198312)
XLA Ops:
  0.0 2.5 %shard_map.38 = bf16[4,8,80,128]{3,2,1,0:T(8,128)(2,1)} custom-call(bf16[256,1024]{1,0:T(8,128)(2,1)} %q_hbm.3, bf16[256,1024]{1,0:T(8,128)(2,1)} %k_hbm.3, bf16[256,1024]{1,0:T(8,128)(2,1)} %v_hbm.3), custom_call_target="tpu_custom_call" | custom-call | bytes 1048576 | tf_op jit(solution)/shard_map/pallas_call | solution.py:253
  2.5 9.2 %all-to-all-start.1 = ((bf16[32,80,128]{2,1,0:T(8,128)(2,1)}), bf16[32,80,128]{2,1,0:T(8,128)(2,1)S(1)}, u32[]{:S(2)}, u32[]{:S(2)}) async-start(bf16[32,80,128]{2,1,0:T(8,128)(2,1)} %bitcast.4), calls=%async_computation.1 | async-start | bytes 1310720 | tf_op jit(solution)/shard_map/all_to_all | solution.py:302
  11.7 2.9 %shard_map.37 = bf16[8,3,256,128]{3,2,1,0:T(8,128)(2,1)} custom-call(bf16[256,1024]{1,0:T(8,128)(2,1)} %q_hbm.3, bf16[256,1024]{1,0:T(8,128)(2,1)} %k_hbm.3, bf16[256,1024]{1,0:T(8,128)(2,1)} %v_hbm.3), custom_call_target="tpu_custom_call" | custom-call | bytes 1048576 | tf_op jit(solution)/shard_map/pallas_call | solution.py:253
  14.6 7.7 %all-to-all-done.1 = bf16[32,80,128]{2,1,0:T(8,128)(2,1)S(1)} async-done(((bf16[32,80,128]{2,1,0:T(8,128)(2,1)}), bf16[32,80,128]{2,1,0:T(8,128)(2,1)S(1)}, u32[]{:S(2)}, u32[]{:S(2)}) %all-to-all-start.1) | async-done | bytes 655392 | tf_op jit(solution)/shard_map/all_to_all | solution.py:302
  22.3 3.6 %all-to-all-start = ((bf16[8,3,256,128]{3,2,1,0:T(8,128)(2,1)}), bf16[8,3,256,128]{3,2,1,0:T(8,128)(2,1)S(1)}, u32[]{:S(2)}, u32[]{:S(2)}) async-start(bf16[8,3,256,128]{3,2,1,0:T(8,128)(2,1)} %shard_map.37), calls=%async_computation | async-start | bytes 3145728 | tf_op jit(solution)/shard_map/all_to_all | solution.py:314
  25.9 0.2 shard_map.39
  26.2 15.0 %collective-permute-start.2 = (bf16[2,128,128]{2,1,0:T(8,128)(2,1)S(1)}, bf16[2,128,128]{2,1,0:T(8,128)(2,1)S(1)}, u32[]{:S(2)}, u32[]{:S(2)}) collective-permute-start(bf16[2,128,128]{2,1,0:T(8,128)(2,1)S(1)} %get-tuple-element.13), channel_id=1, source_target_pairs={{0,256},{8,264},{16,80},{24,88},{32,160},{40,168},{48,240},{56,248... | collective-permute-start | bytes 196616 | tf_op jit(solution)/shard_map/ppermute | solution.py:323
  41.2 0.7 collective-permute-start.3
  41.8 4.9 %collective-permute-start.1 = (bf16[128,128]{1,0:T(8,128)(2,1)S(1)}, bf16[128,128]{1,0:T(8,128)(2,1)S(1)}, u32[]{:S(2)}, u32[]{:S(2)}) collective-permute-start(bf16[128,128]{1,0:T(8,128)(2,1)S(1)} %get-tuple-element.12.here_ref), channel_id=1, source_target_pairs={{0,8},{8,0},{16,24},{24,16},{32,40},{40,32},{48,56},{56,48},{64,72... | collective-permute-start | bytes 98312 | tf_op jit(solution)/shard_map/ppermute | solution.py:326
  46.8 1.9 %collective-permute-start = (bf16[4,8,64,128]{3,2,1,0:T(8,128)(2,1)S(1)}, bf16[4,8,64,128]{3,2,1,0:T(8,128)(2,1)S(1)}, u32[]{:S(2)}, u32[]{:S(2)}) collective-permute-start(bf16[4,8,64,128]{3,2,1,0:T(8,128)(2,1)S(1)} %get-tuple-element.10.here_ref), channel_id=1, source_target_pairs={{0,8},{8,0},{16,24},{24,16},{32,40},{40,32},{48,56},{56,48},{64,72... | collective-permute-start | bytes 1572872 | tf_op jit(solution)/shard_map/ppermute | solution.py:327
  48.7 0.0 collective-permute-done.1.there_ref
  48.7 0.0 collective-permute-done.2.far_a
  48.7 0.0 collective-permute-done.3.far_b
  48.7 1.3 %shard_map.41 = f32[8,8,8,128]{3,2,1,0:T(8,128)} custom-call(s32[1]{0:T(128)} %bitcast.2.core_ref, bf16[128,128]{1,0:T(8,128)(2,1)S(1)} %get-tuple-element.12.here_ref, bf16[128,128]{1,0:T(8,128)(2,1)S(1)} %collective-permute-done.1.there_ref, bf16[2,128,128]{2,1,0:T(8,128)(2,1)S(1)} %collective-permute-done.2.far_a, ...), custom_call_target="tpu_custom_call" | custom-call | flops 4294967296 | bytes 1048576 | tf_op jit(solution)/shard_map/pallas_call | solution.py:253
  50.0 0.0 all-to-all-done.qkv_ref
  50.0 5.1 %all-to-all-start.2 = ((f32[8,8,8,128]{3,2,1,0:T(8,128)}), f32[8,8,8,128]{3,2,1,0:T(8,128)S(1)}, u32[]{:S(2)}, u32[]{:S(2)}) async-start(f32[8,8,8,128]{3,2,1,0:T(8,128)} %shard_map.41), calls=%async_computation.2 | async-start | bytes 524288 | tf_op jit(solution)/shard_map/all_to_all | solution.py:337
  55.2 0.0 collective-permute-done.there_hbm
  55.2 6.0 %shard_map.40 = (bf16[8,256,128]{2,1,0:T(8,128)(2,1)S(1)}, f32[8,8,128]{2,1,0:T(8,128)S(1)}) custom-call(bf16[8,3,256,128]{3,2,1,0:T(8,128)(2,1)S(1)} %all-to-all-done.qkv_ref, bf16[4,8,64,128]{3,2,1,0:T(8,128)(2,1)S(1)} %get-tuple-element.10.here_ref, bf16[4,8,64,128]{3,2,1,0:T(8,128)(2,1)S(1)} %collective-permute-done.there_hbm), custom_call_target="tpu_custom_call" | custom-call | flops 8589934592 | bytes 1048576 | tf_op jit(solution)/shard_map/pallas_call | solution.py:253
  61.2 0.4 all-to-all-done.2.third_ref
  61.6 0.1 shard_map.42
  61.7 13.5 %all_to_all.20.o_ref = bf16[8,256,128]{2,1,0:T(8,128)(2,1)S(1)} all-to-all(bf16[8,256,128]{2,1,0:T(8,128)(2,1)S(1)} %shard_map.42), channel_id=1, replica_groups=mesh['outer'=64,'inner'=8] {'inner'}, dimensions={0} | all-to-all | bytes 1048576 | tf_op jit(solution)/shard_map/all_to_all | solution.py:357
  75.2 1.2 %shard_map.43 = bf16[256,1024]{1,0:T(8,128)(2,1)} custom-call(bf16[8,256,128]{2,1,0:T(8,128)(2,1)S(1)} %all_to_all.20.o_ref), custom_call_target="tpu_custom_call" | custom-call | bytes 1048576 | tf_op jit(solution)/shard_map/pallas_call | solution.py:253
Async XLA Ops:
  2.5 19.9 %all-to-all-start.1 = ((bf16[32,80,128]{2,1,0:T(8,128)(2,1)}), bf16[32,80,128]{2,1,0:T(8,128)(2,1)S(1)}, u32[]{:S(2)}, u32[]{:S(2)}) async-start(bf16[32,80,128]{2,1,0:T(8,128)(2,1)} %bitcast.4), calls=%async_computation.1 | async-start | bytes 1310720 | tf_op jit(solution)/shard_map/all_to_all | solution.py:302
  22.3 27.7 %all-to-all-start = ((bf16[8,3,256,128]{3,2,1,0:T(8,128)(2,1)}), bf16[8,3,256,128]{3,2,1,0:T(8,128)(2,1)S(1)}, u32[]{:S(2)}, u32[]{:S(2)}) async-start(bf16[8,3,256,128]{3,2,1,0:T(8,128)(2,1)} %shard_map.37), calls=%async_computation | async-start | bytes 3145728 | tf_op jit(solution)/shard_map/all_to_all | solution.py:314
  26.2 22.5 %collective-permute-start.2 = (bf16[2,128,128]{2,1,0:T(8,128)(2,1)S(1)}, bf16[2,128,128]{2,1,0:T(8,128)(2,1)S(1)}, u32[]{:S(2)}, u32[]{:S(2)}) collective-permute-start(bf16[2,128,128]{2,1,0:T(8,128)(2,1)S(1)} %get-tuple-element.13), channel_id=1, source_target_pairs={{0,256},{8,264},{16,80},{24,88},{32,160},{40,168},{48,240},{56,248... | collective-permute-start | bytes 196616 | tf_op jit(solution)/shard_map/ppermute | solution.py:323
  41.2 7.5 %collective-permute-start.3 = (bf16[2,128,128]{2,1,0:T(8,128)(2,1)S(1)}, bf16[2,128,128]{2,1,0:T(8,128)(2,1)S(1)}, u32[]{:S(2)}, u32[]{:S(2)}) collective-permute-start(bf16[2,128,128]{2,1,0:T(8,128)(2,1)S(1)} %get-tuple-element.13), channel_id=1, source_target_pairs={{0,0},{8,8},{16,336},{24,344},{32,416},{40,424},{48,496},{56,504},... | collective-permute-start | bytes 196616 | tf_op jit(solution)/shard_map/ppermute | solution.py:323
  41.8 6.9 %collective-permute-start.1 = (bf16[128,128]{1,0:T(8,128)(2,1)S(1)}, bf16[128,128]{1,0:T(8,128)(2,1)S(1)}, u32[]{:S(2)}, u32[]{:S(2)}) collective-permute-start(bf16[128,128]{1,0:T(8,128)(2,1)S(1)} %get-tuple-element.12.here_ref), channel_id=1, source_target_pairs={{0,8},{8,0},{16,24},{24,16},{32,40},{40,32},{48,56},{56,48},{64,72... | collective-permute-start | bytes 98312 | tf_op jit(solution)/shard_map/ppermute | solution.py:326
  46.8 8.4 %collective-permute-start = (bf16[4,8,64,128]{3,2,1,0:T(8,128)(2,1)S(1)}, bf16[4,8,64,128]{3,2,1,0:T(8,128)(2,1)S(1)}, u32[]{:S(2)}, u32[]{:S(2)}) collective-permute-start(bf16[4,8,64,128]{3,2,1,0:T(8,128)(2,1)S(1)} %get-tuple-element.10.here_ref), channel_id=1, source_target_pairs={{0,8},{8,0},{16,24},{24,16},{32,40},{40,32},{48,56},{56,48},{64,72... | collective-permute-start | bytes 1572872 | tf_op jit(solution)/shard_map/ppermute | solution.py:327
  50.0 11.5 %all-to-all-start.2 = ((f32[8,8,8,128]{3,2,1,0:T(8,128)}), f32[8,8,8,128]{3,2,1,0:T(8,128)S(1)}, u32[]{:S(2)}, u32[]{:S(2)}) async-start(f32[8,8,8,128]{3,2,1,0:T(8,128)} %shard_map.41), calls=%async_computation.2 | async-start | bytes 524288 | tf_op jit(solution)/shard_map/all_to_all | solution.py:337

commit v7 on v6

--- a/solution.py
+++ b/solution.py
@@ -321,7 +321,7 @@
     place = [(g, j) for g in range(groups) for j in range(NEAR)]
     far_a, far_b = [
         lax.ppermute(far, "outer", [(g * NEAR + j, (g + by[j // 2]) % groups * NEAR + j) for g, j in place])
-        for by in ((4, 1, 2, 3), (0, 5, 6, 7))
+        for by in ((4, 3, 5, 2), (0, 7, 1, 6))
     ]
     q3_there = lax.ppermute(q3_here, "outer", other_core)
     there = lax.ppermute(here, "outer", other_core)

time: 77.7 us -> 78.1 us (level)
  no operation moved by 1% of the time
where the time goes in v7:
time: 78.1 us; the launch traced here: 76.8 us
  starting transfers between devices  40.3 us (52%)
  Pallas kernels  14.2 us (18%)
  blocking collectives  14 us (18%)
  waiting for transfers between devices  8.13 us (10%)
    ppermute x2, starting transfers between devices, body(): lax.ppermute(far, 'outer', [(g * NEAR + j, (g + by[j // 2]) % groups * NE...  15.7 us
    pallas_call x7, Pallas kernels, call(): pl.pallas_call(kernel, out_shape=shapes, in_specs=in_specs or vmem(len(in...  14.2 us
    all_to_all x1, blocking collectives, body(): o = lax.all_to_all(o, 'inner', 0, 0, tiled=True)  14 us
    all_to_all x1, starting transfers between devices, body(): lax.all_to_all(near, ('outer', 'inner'), 0, 0, tiled=True, axis_index_gro...  9.23 us
    all_to_all x1, waiting for transfers between devices, body(): lax.all_to_all(near, ('outer', 'inner'), 0, 0, tiled=True, axis_index_gro...  7.7 us
    all_to_all x1, starting transfers between devices, body(): lax.all_to_all(third, 'outer', 0, 0, tiled=True, axis_index_groups=near_g...  5.02 us
    ppermute x1, starting transfers between devices, body(): q3_there = lax.ppermute(q3_here, 'outer', other_core)  4.91 us
    all_to_all x1, starting transfers between devices, body(): qkv = lax.all_to_all(qkv, 'inner', 0, 0, tiled=True)  3.58 us
  transfers between devices with their start and end apart: 7, of which 2 were waited for; matrix products, arithmetic and copies ran while one was open for 0% of the time, Pallas kernels for 14%

profile of v7, /device:TPU:1, one launch (start us, length us, event | category | flops | bytes accessed | tf_op | source)
XLA Modules:
  0.0 76.8 jit_solution(8366729855009841073)
XLA Ops:
  0.0 2.5 %shard_map.38 = bf16[4,8,80,128]{3,2,1,0:T(8,128)(2,1)} custom-call(bf16[256,1024]{1,0:T(8,128)(2,1)} %q_hbm.3, bf16[256,1024]{1,0:T(8,128)(2,1)} %k_hbm.3, bf16[256,1024]{1,0:T(8,128)(2,1)} %v_hbm.3), custom_call_target="tpu_custom_call" | custom-call | bytes 1048576 | tf_op jit(solution)/shard_map/pallas_call | solution.py:253
  2.5 9.2 %all-to-all-start.1 = ((bf16[32,80,128]{2,1,0:T(8,128)(2,1)}), bf16[32,80,128]{2,1,0:T(8,128)(2,1)S(1)}, u32[]{:S(2)}, u32[]{:S(2)}) async-start(bf16[32,80,128]{2,1,0:T(8,128)(2,1)} %bitcast.4), calls=%async_computation.1 | async-start | bytes 1310720 | tf_op jit(solution)/shard_map/all_to_all | solution.py:302
  11.7 2.9 %shard_map.37 = bf16[8,3,256,128]{3,2,1,0:T(8,128)(2,1)} custom-call(bf16[256,1024]{1,0:T(8,128)(2,1)} %q_hbm.3, bf16[256,1024]{1,0:T(8,128)(2,1)} %k_hbm.3, bf16[256,1024]{1,0:T(8,128)(2,1)} %v_hbm.3), custom_call_target="tpu_custom_call" | custom-call | bytes 1048576 | tf_op jit(solution)/shard_map/pallas_call | solution.py:253
  14.6 7.7 %all-to-all-done.1 = bf16[32,80,128]{2,1,0:T(8,128)(2,1)S(1)} async-done(((bf16[32,80,128]{2,1,0:T(8,128)(2,1)}), bf16[32,80,128]{2,1,0:T(8,128)(2,1)S(1)}, u32[]{:S(2)}, u32[]{:S(2)}) %all-to-all-start.1) | async-done | bytes 655392 | tf_op jit(solution)/shard_map/all_to_all | solution.py:302
  22.3 3.6 %all-to-all-start = ((bf16[8,3,256,128]{3,2,1,0:T(8,128)(2,1)}), bf16[8,3,256,128]{3,2,1,0:T(8,128)(2,1)S(1)}, u32[]{:S(2)}, u32[]{:S(2)}) async-start(bf16[8,3,256,128]{3,2,1,0:T(8,128)(2,1)} %shard_map.37), calls=%async_computation | async-start | bytes 3145728 | tf_op jit(solution)/shard_map/all_to_all | solution.py:314
  25.9 0.2 shard_map.39
  26.2 15.0 %collective-permute-start.2 = (bf16[2,128,128]{2,1,0:T(8,128)(2,1)S(1)}, bf16[2,128,128]{2,1,0:T(8,128)(2,1)S(1)}, u32[]{:S(2)}, u32[]{:S(2)}) collective-permute-start(bf16[2,128,128]{2,1,0:T(8,128)(2,1)S(1)} %get-tuple-element.13), channel_id=1, source_target_pairs={{0,256},{8,264},{16,208},{24,216},{32,352},{40,360},{48,176},{56,1... | collective-permute-start | bytes 196616 | tf_op jit(solution)/shard_map/ppermute | solution.py:323
  41.2 0.7 collective-permute-start.3
  41.8 4.9 %collective-permute-start.1 = (bf16[128,128]{1,0:T(8,128)(2,1)S(1)}, bf16[128,128]{1,0:T(8,128)(2,1)S(1)}, u32[]{:S(2)}, u32[]{:S(2)}) collective-permute-start(bf16[128,128]{1,0:T(8,128)(2,1)S(1)} %get-tuple-element.12.here_ref), channel_id=1, source_target_pairs={{0,8},{8,0},{16,24},{24,16},{32,40},{40,32},{48,56},{56,48},{64,72... | collective-permute-start | bytes 98312 | tf_op jit(solution)/shard_map/ppermute | solution.py:326
  46.8 1.9 %collective-permute-start = (bf16[4,8,64,128]{3,2,1,0:T(8,128)(2,1)S(1)}, bf16[4,8,64,128]{3,2,1,0:T(8,128)(2,1)S(1)}, u32[]{:S(2)}, u32[]{:S(2)}) collective-permute-start(bf16[4,8,64,128]{3,2,1,0:T(8,128)(2,1)S(1)} %get-tuple-element.10.here_ref), channel_id=1, source_target_pairs={{0,8},{8,0},{16,24},{24,16},{32,40},{40,32},{48,56},{56,48},{64,72... | collective-permute-start | bytes 1572872 | tf_op jit(solution)/shard_map/ppermute | solution.py:327
  48.7 0.0 collective-permute-done.1.there_ref
  48.7 0.0 collective-permute-done.2.far_a
  48.7 0.0 collective-permute-done.3.far_b
  48.7 1.3 %shard_map.41 = f32[8,8,8,128]{3,2,1,0:T(8,128)} custom-call(s32[1]{0:T(128)} %bitcast.2.core_ref, bf16[128,128]{1,0:T(8,128)(2,1)S(1)} %get-tuple-element.12.here_ref, bf16[128,128]{1,0:T(8,128)(2,1)S(1)} %collective-permute-done.1.there_ref, bf16[2,128,128]{2,1,0:T(8,128)(2,1)S(1)} %collective-permute-done.2.far_a, ...), custom_call_target="tpu_custom_call" | custom-call | flops 4294967296 | bytes 1048576 | tf_op jit(solution)/shard_map/pallas_call | solution.py:253
  50.0 0.0 all-to-all-done.qkv_ref
  50.0 5.0 %all-to-all-start.2 = ((f32[8,8,8,128]{3,2,1,0:T(8,128)}), f32[8,8,8,128]{3,2,1,0:T(8,128)S(1)}, u32[]{:S(2)}, u32[]{:S(2)}) async-start(f32[8,8,8,128]{3,2,1,0:T(8,128)} %shard_map.41), calls=%async_computation.2 | async-start | bytes 524288 | tf_op jit(solution)/shard_map/all_to_all | solution.py:337
  55.1 0.0 collective-permute-done.there_hbm
  55.1 6.0 %shard_map.40 = (bf16[8,256,128]{2,1,0:T(8,128)(2,1)S(1)}, f32[8,8,128]{2,1,0:T(8,128)S(1)}) custom-call(bf16[8,3,256,128]{3,2,1,0:T(8,128)(2,1)S(1)} %all-to-all-done.qkv_ref, bf16[4,8,64,128]{3,2,1,0:T(8,128)(2,1)S(1)} %get-tuple-element.10.here_ref, bf16[4,8,64,128]{3,2,1,0:T(8,128)(2,1)S(1)} %collective-permute-done.there_hbm), custom_call_target="tpu_custom_call" | custom-call | flops 8589934592 | bytes 1048576 | tf_op jit(solution)/shard_map/pallas_call | solution.py:253
  61.1 0.4 all-to-all-done.2.third_ref
  61.5 0.1 shard_map.42
  61.6 14.0 %all_to_all.20.o_ref = bf16[8,256,128]{2,1,0:T(8,128)(2,1)S(1)} all-to-all(bf16[8,256,128]{2,1,0:T(8,128)(2,1)S(1)} %shard_map.42), channel_id=1, replica_groups=mesh['outer'=64,'inner'=8] {'inner'}, dimensions={0} | all-to-all | bytes 1048576 | tf_op jit(solution)/shard_map/all_to_all | solution.py:357
  75.6 1.2 %shard_map.43 = bf16[256,1024]{1,0:T(8,128)(2,1)} custom-call(bf16[8,256,128]{2,1,0:T(8,128)(2,1)S(1)} %all_to_all.20.o_ref), custom_call_target="tpu_custom_call" | custom-call | bytes 1048576 | tf_op jit(solution)/shard_map/pallas_call | solution.py:253
Async XLA Ops:
  2.5 19.9 %all-to-all-start.1 = ((bf16[32,80,128]{2,1,0:T(8,128)(2,1)}), bf16[32,80,128]{2,1,0:T(8,128)(2,1)S(1)}, u32[]{:S(2)}, u32[]{:S(2)}) async-start(bf16[32,80,128]{2,1,0:T(8,128)(2,1)} %bitcast.4), calls=%async_computation.1 | async-start | bytes 1310720 | tf_op jit(solution)/shard_map/all_to_all | solution.py:302
  22.3 27.7 %all-to-all-start = ((bf16[8,3,256,128]{3,2,1,0:T(8,128)(2,1)}), bf16[8,3,256,128]{3,2,1,0:T(8,128)(2,1)S(1)}, u32[]{:S(2)}, u32[]{:S(2)}) async-start(bf16[8,3,256,128]{3,2,1,0:T(8,128)(2,1)} %shard_map.37), calls=%async_computation | async-start | bytes 3145728 | tf_op jit(solution)/shard_map/all_to_all | solution.py:314
  26.2 22.5 %collective-permute-start.2 = (bf16[2,128,128]{2,1,0:T(8,128)(2,1)S(1)}, bf16[2,128,128]{2,1,0:T(8,128)(2,1)S(1)}, u32[]{:S(2)}, u32[]{:S(2)}) collective-permute-start(bf16[2,128,128]{2,1,0:T(8,128)(2,1)S(1)} %get-tuple-element.13), channel_id=1, source_target_pairs={{0,256},{8,264},{16,208},{24,216},{32,352},{40,360},{48,176},{56,1... | collective-permute-start | bytes 196616 | tf_op jit(solution)/shard_map/ppermute | solution.py:323
  41.2 7.5 %collective-permute-start.3 = (bf16[2,128,128]{2,1,0:T(8,128)(2,1)S(1)}, bf16[2,128,128]{2,1,0:T(8,128)(2,1)S(1)}, u32[]{:S(2)}, u32[]{:S(2)}) collective-permute-start(bf16[2,128,128]{2,1,0:T(8,128)(2,1)S(1)} %get-tuple-element.13), channel_id=1, source_target_pairs={{0,0},{8,8},{16,464},{24,472},{32,96},{40,104},{48,432},{56,440},{... | collective-permute-start | bytes 196616 | tf_op jit(solution)/shard_map/ppermute | solution.py:323
  41.8 6.9 %collective-permute-start.1 = (bf16[128,128]{1,0:T(8,128)(2,1)S(1)}, bf16[128,128]{1,0:T(8,128)(2,1)S(1)}, u32[]{:S(2)}, u32[]{:S(2)}) collective-permute-start(bf16[128,128]{1,0:T(8,128)(2,1)S(1)} %get-tuple-element.12.here_ref), channel_id=1, source_target_pairs={{0,8},{8,0},{16,24},{24,16},{32,40},{40,32},{48,56},{56,48},{64,72... | collective-permute-start | bytes 98312 | tf_op jit(solution)/shard_map/ppermute | solution.py:326
  46.8 8.3 %collective-permute-start = (bf16[4,8,64,128]{3,2,1,0:T(8,128)(2,1)S(1)}, bf16[4,8,64,128]{3,2,1,0:T(8,128)(2,1)S(1)}, u32[]{:S(2)}, u32[]{:S(2)}) collective-permute-start(bf16[4,8,64,128]{3,2,1,0:T(8,128)(2,1)S(1)} %get-tuple-element.10.here_ref), channel_id=1, source_target_pairs={{0,8},{8,0},{16,24},{24,16},{32,40},{40,32},{48,56},{56,48},{64,72... | collective-permute-start | bytes 1572872 | tf_op jit(solution)/shard_map/ppermute | solution.py:327
  50.0 11.4 %all-to-all-start.2 = ((f32[8,8,8,128]{3,2,1,0:T(8,128)}), f32[8,8,8,128]{3,2,1,0:T(8,128)S(1)}, u32[]{:S(2)}, u32[]{:S(2)}) async-start(f32[8,8,8,128]{3,2,1,0:T(8,128)} %shard_map.41), calls=%async_computation.2 | async-start | bytes 524288 | tf_op jit(solution)/shard_map/all_to_all | solution.py:337

commit v8 on v7

--- a/solution.py
+++ b/solution.py
@@ -321,7 +321,7 @@
     place = [(g, j) for g in range(groups) for j in range(NEAR)]
     far_a, far_b = [
         lax.ppermute(far, "outer", [(g * NEAR + j, (g + by[j // 2]) % groups * NEAR + j) for g, j in place])
-        for by in ((4, 3, 5, 2), (0, 7, 1, 6))
+        for by in ((0, 1, 2, 3), (4, 5, 6, 7))
     ]
     q3_there = lax.ppermute(q3_here, "outer", other_core)
     there = lax.ppermute(here, "outer", other_core)

time: 78.1 us -> 77.7 us (level)
  no operation moved by 1% of the time
where the time goes in v8:
time: 77.7 us; the launch traced here: 76.3 us
  starting transfers between devices  40.4 us (52%)
  Pallas kernels  14.2 us (18%)
  blocking collectives  13.5 us (17%)
  waiting for transfers between devices  8.12 us (10%)
    ppermute x2, starting transfers between devices, body(): lax.ppermute(far, 'outer', [(g * NEAR + j, (g + by[j // 2]) % groups * NE...  15.7 us
    pallas_call x7, Pallas kernels, call(): pl.pallas_call(kernel, out_shape=shapes, in_specs=in_specs or vmem(len(in...  14.2 us
    all_to_all x1, blocking collectives, body(): o = lax.all_to_all(o, 'inner', 0, 0, tiled=True)  13.5 us
    all_to_all x1, starting transfers between devices, body(): lax.all_to_all(near, ('outer', 'inner'), 0, 0, tiled=True, axis_index_gro...  9.23 us
    all_to_all x1, waiting for transfers between devices, body(): lax.all_to_all(near, ('outer', 'inner'), 0, 0, tiled=True, axis_index_gro...  7.7 us
    all_to_all x1, starting transfers between devices, body(): lax.all_to_all(third, 'outer', 0, 0, tiled=True, axis_index_groups=near_g...  5.12 us
    ppermute x1, starting transfers between devices, body(): q3_there = lax.ppermute(q3_here, 'outer', other_core)  4.91 us
    all_to_all x1, starting transfers between devices, body(): qkv = lax.all_to_all(qkv, 'inner', 0, 0, tiled=True)  3.58 us
  transfers between devices with their start and end apart: 7, of which 2 were waited for; matrix products, arithmetic and copies ran while one was open for 0% of the time, Pallas kernels for 14%

profile of v8, /device:TPU:1, one launch (start us, length us, event | category | flops | bytes accessed | tf_op | source)
XLA Modules:
  0.0 76.3 jit_solution(32111510870771152)
XLA Ops:
  0.0 2.5 %shard_map.38 = bf16[4,8,80,128]{3,2,1,0:T(8,128)(2,1)} custom-call(bf16[256,1024]{1,0:T(8,128)(2,1)} %q_hbm.3, bf16[256,1024]{1,0:T(8,128)(2,1)} %k_hbm.3, bf16[256,1024]{1,0:T(8,128)(2,1)} %v_hbm.3), custom_call_target="tpu_custom_call" | custom-call | bytes 1048576 | tf_op jit(solution)/shard_map/pallas_call | solution.py:253
  2.5 9.2 %all-to-all-start.1 = ((bf16[32,80,128]{2,1,0:T(8,128)(2,1)}), bf16[32,80,128]{2,1,0:T(8,128)(2,1)S(1)}, u32[]{:S(2)}, u32[]{:S(2)}) async-start(bf16[32,80,128]{2,1,0:T(8,128)(2,1)} %bitcast.4), calls=%async_computation.1 | async-start | bytes 1310720 | tf_op jit(solution)/shard_map/all_to_all | solution.py:302
  11.7 2.9 %shard_map.37 = bf16[8,3,256,128]{3,2,1,0:T(8,128)(2,1)} custom-call(bf16[256,1024]{1,0:T(8,128)(2,1)} %q_hbm.3, bf16[256,1024]{1,0:T(8,128)(2,1)} %k_hbm.3, bf16[256,1024]{1,0:T(8,128)(2,1)} %v_hbm.3), custom_call_target="tpu_custom_call" | custom-call | bytes 1048576 | tf_op jit(solution)/shard_map/pallas_call | solution.py:253
  14.6 7.7 %all-to-all-done.1 = bf16[32,80,128]{2,1,0:T(8,128)(2,1)S(1)} async-done(((bf16[32,80,128]{2,1,0:T(8,128)(2,1)}), bf16[32,80,128]{2,1,0:T(8,128)(2,1)S(1)}, u32[]{:S(2)}, u32[]{:S(2)}) %all-to-all-start.1) | async-done | bytes 655392 | tf_op jit(solution)/shard_map/all_to_all | solution.py:302
  22.3 3.6 %all-to-all-start = ((bf16[8,3,256,128]{3,2,1,0:T(8,128)(2,1)}), bf16[8,3,256,128]{3,2,1,0:T(8,128)(2,1)S(1)}, u32[]{:S(2)}, u32[]{:S(2)}) async-start(bf16[8,3,256,128]{3,2,1,0:T(8,128)(2,1)} %shard_map.37), calls=%async_computation | async-start | bytes 3145728 | tf_op jit(solution)/shard_map/all_to_all | solution.py:314
  25.9 0.2 shard_map.39
  26.2 0.7 collective-permute-start.2
  26.8 15.0 %collective-permute-start.3 = (bf16[2,128,128]{2,1,0:T(8,128)(2,1)S(1)}, bf16[2,128,128]{2,1,0:T(8,128)(2,1)S(1)}, u32[]{:S(2)}, u32[]{:S(2)}) collective-permute-start(bf16[2,128,128]{2,1,0:T(8,128)(2,1)S(1)} %get-tuple-element.13), channel_id=1, source_target_pairs={{0,256},{8,264},{16,336},{24,344},{32,416},{40,424},{48,496},{56,5... | collective-permute-start | bytes 196616 | tf_op jit(solution)/shard_map/ppermute | solution.py:323
  41.8 4.9 %collective-permute-start.1 = (bf16[128,128]{1,0:T(8,128)(2,1)S(1)}, bf16[128,128]{1,0:T(8,128)(2,1)S(1)}, u32[]{:S(2)}, u32[]{:S(2)}) collective-permute-start(bf16[128,128]{1,0:T(8,128)(2,1)S(1)} %get-tuple-element.12.here_ref), channel_id=1, source_target_pairs={{0,8},{8,0},{16,24},{24,16},{32,40},{40,32},{48,56},{56,48},{64,72... | collective-permute-start | bytes 98312 | tf_op jit(solution)/shard_map/ppermute | solution.py:326
  46.8 1.9 %collective-permute-start = (bf16[4,8,64,128]{3,2,1,0:T(8,128)(2,1)S(1)}, bf16[4,8,64,128]{3,2,1,0:T(8,128)(2,1)S(1)}, u32[]{:S(2)}, u32[]{:S(2)}) collective-permute-start(bf16[4,8,64,128]{3,2,1,0:T(8,128)(2,1)S(1)} %get-tuple-element.10.here_ref), channel_id=1, source_target_pairs={{0,8},{8,0},{16,24},{24,16},{32,40},{40,32},{48,56},{56,48},{64,72... | collective-permute-start | bytes 1572872 | tf_op jit(solution)/shard_map/ppermute | solution.py:327
  48.7 0.0 collective-permute-done.1.there_ref
  48.7 0.0 collective-permute-done.2.far_a
  48.7 0.0 collective-permute-done.3.far_b
  48.7 1.3 %shard_map.41 = f32[8,8,8,128]{3,2,1,0:T(8,128)} custom-call(s32[1]{0:T(128)} %bitcast.2.core_ref, bf16[128,128]{1,0:T(8,128)(2,1)S(1)} %get-tuple-element.12.here_ref, bf16[128,128]{1,0:T(8,128)(2,1)S(1)} %collective-permute-done.1.there_ref, bf16[2,128,128]{2,1,0:T(8,128)(2,1)S(1)} %collective-permute-done.2.far_a, ...), custom_call_target="tpu_custom_call" | custom-call | flops 4294967296 | bytes 1048576 | tf_op jit(solution)/shard_map/pallas_call | solution.py:253
  50.0 0.0 all-to-all-done.qkv_ref
  50.0 5.1 %all-to-all-start.2 = ((f32[8,8,8,128]{3,2,1,0:T(8,128)}), f32[8,8,8,128]{3,2,1,0:T(8,128)S(1)}, u32[]{:S(2)}, u32[]{:S(2)}) async-start(f32[8,8,8,128]{3,2,1,0:T(8,128)} %shard_map.41), calls=%async_computation.2 | async-start | bytes 524288 | tf_op jit(solution)/shard_map/all_to_all | solution.py:337
  55.2 0.0 collective-permute-done.there_hbm
  55.2 6.0 %shard_map.40 = (bf16[8,256,128]{2,1,0:T(8,128)(2,1)S(1)}, f32[8,8,128]{2,1,0:T(8,128)S(1)}) custom-call(bf16[8,3,256,128]{3,2,1,0:T(8,128)(2,1)S(1)} %all-to-all-done.qkv_ref, bf16[4,8,64,128]{3,2,1,0:T(8,128)(2,1)S(1)} %get-tuple-element.10.here_ref, bf16[4,8,64,128]{3,2,1,0:T(8,128)(2,1)S(1)} %collective-permute-done.there_hbm), custom_call_target="tpu_custom_call" | custom-call | flops 8589934592 | bytes 1048576 | tf_op jit(solution)/shard_map/pallas_call | solution.py:253
  61.2 0.4 all-to-all-done.2.third_ref
  61.6 0.1 shard_map.42
  61.7 13.5 %all_to_all.20.o_ref = bf16[8,256,128]{2,1,0:T(8,128)(2,1)S(1)} all-to-all(bf16[8,256,128]{2,1,0:T(8,128)(2,1)S(1)} %shard_map.42), channel_id=1, replica_groups=mesh['outer'=64,'inner'=8] {'inner'}, dimensions={0} | all-to-all | bytes 1048576 | tf_op jit(solution)/shard_map/all_to_all | solution.py:357
  75.2 1.2 %shard_map.43 = bf16[256,1024]{1,0:T(8,128)(2,1)} custom-call(bf16[8,256,128]{2,1,0:T(8,128)(2,1)S(1)} %all_to_all.20.o_ref), custom_call_target="tpu_custom_call" | custom-call | bytes 1048576 | tf_op jit(solution)/shard_map/pallas_call | solution.py:253
Async XLA Ops:
  2.5 19.9 %all-to-all-start.1 = ((bf16[32,80,128]{2,1,0:T(8,128)(2,1)}), bf16[32,80,128]{2,1,0:T(8,128)(2,1)S(1)}, u32[]{:S(2)}, u32[]{:S(2)}) async-start(bf16[32,80,128]{2,1,0:T(8,128)(2,1)} %bitcast.4), calls=%async_computation.1 | async-start | bytes 1310720 | tf_op jit(solution)/shard_map/all_to_all | solution.py:302
  22.3 27.7 %all-to-all-start = ((bf16[8,3,256,128]{3,2,1,0:T(8,128)(2,1)}), bf16[8,3,256,128]{3,2,1,0:T(8,128)(2,1)S(1)}, u32[]{:S(2)}, u32[]{:S(2)}) async-start(bf16[8,3,256,128]{3,2,1,0:T(8,128)(2,1)} %shard_map.37), calls=%async_computation | async-start | bytes 3145728 | tf_op jit(solution)/shard_map/all_to_all | solution.py:314
  26.2 22.5 %collective-permute-start.2 = (bf16[2,128,128]{2,1,0:T(8,128)(2,1)S(1)}, bf16[2,128,128]{2,1,0:T(8,128)(2,1)S(1)}, u32[]{:S(2)}, u32[]{:S(2)}) collective-permute-start(bf16[2,128,128]{2,1,0:T(8,128)(2,1)S(1)} %get-tuple-element.13), channel_id=1, source_target_pairs={{0,0},{8,8},{16,80},{24,88},{32,160},{40,168},{48,240},{56,248},{6... | collective-permute-start | bytes 196616 | tf_op jit(solution)/shard_map/ppermute | solution.py:323
  26.8 21.9 %collective-permute-start.3 = (bf16[2,128,128]{2,1,0:T(8,128)(2,1)S(1)}, bf16[2,128,128]{2,1,0:T(8,128)(2,1)S(1)}, u32[]{:S(2)}, u32[]{:S(2)}) collective-permute-start(bf16[2,128,128]{2,1,0:T(8,128)(2,1)S(1)} %get-tuple-element.13), channel_id=1, source_target_pairs={{0,256},{8,264},{16,336},{24,344},{32,416},{40,424},{48,496},{56,5... | collective-permute-start | bytes 196616 | tf_op jit(solution)/shard_map/ppermute | solution.py:323
  41.8 6.9 %collective-permute-start.1 = (bf16[128,128]{1,0:T(8,128)(2,1)S(1)}, bf16[128,128]{1,0:T(8,128)(2,1)S(1)}, u32[]{:S(2)}, u32[]{:S(2)}) collective-permute-start(bf16[128,128]{1,0:T(8,128)(2,1)S(1)} %get-tuple-element.12.here_ref), channel_id=1, source_target_pairs={{0,8},{8,0},{16,24},{24,16},{32,40},{40,32},{48,56},{56,48},{64,72... | collective-permute-start | bytes 98312 | tf_op jit(solution)/shard_map/ppermute | solution.py:326
  46.8 8.4 %collective-permute-start = (bf16[4,8,64,128]{3,2,1,0:T(8,128)(2,1)S(1)}, bf16[4,8,64,128]{3,2,1,0:T(8,128)(2,1)S(1)}, u32[]{:S(2)}, u32[]{:S(2)}) collective-permute-start(bf16[4,8,64,128]{3,2,1,0:T(8,128)(2,1)S(1)} %get-tuple-element.10.here_ref), channel_id=1, source_target_pairs={{0,8},{8,0},{16,24},{24,16},{32,40},{40,32},{48,56},{56,48},{64,72... | collective-permute-start | bytes 1572872 | tf_op jit(solution)/shard_map/ppermute | solution.py:327
  50.0 11.5 %all-to-all-start.2 = ((f32[8,8,8,128]{3,2,1,0:T(8,128)}), f32[8,8,8,128]{3,2,1,0:T(8,128)S(1)}, u32[]{:S(2)}, u32[]{:S(2)}) async-start(f32[8,8,8,128]{3,2,1,0:T(8,128)} %shard_map.41), calls=%async_computation.2 | async-start | bytes 524288 | tf_op jit(solution)/shard_map/all_to_all | solution.py:337
